TPU v7x, 256 devices: a whole 4x4x8 slice. The times are simulated.
256 devices in a mesh: dp: 16 (over x, z_hi), mp: 4 (over y), pre: 4 (over z_lo, core).
Axes of the slice: x: 4, y: 4, z: 8 (z_hi: 4, z_lo: 2; z = z_hi * 2 + z_lo), core: 2. Of those that a mesh axis runs over, the one named last changes fastest.
Arguments:
- activations: bfloat16 [4096, 16384], P('dp', 'mp'), may hold values from -12.7 to 12.7
- cotangent: bfloat16 [4096, 4096], P('dp', 'pre'), may hold values from -12.7 to 12.7
- weight_blocks: bfloat16 [16, 4, 4, 512, 512], P('dp', 'mp', 'pre'), may hold values from -0.09375 to 0.09375
- left_stat: float32 [16, 4, 4, 512, 512], P('dp', 'mp', 'pre'), may hold values from -0.01875 to 0.8625, as said below
- right_stat: float32 [16, 4, 4, 512, 512], P('dp', 'mp', 'pre'), may hold values from -0.01875 to 0.8625, as said below
Outputs:
- input_grad: bfloat16 [4096, 16384], P('dp', ('mp', 'pre'))
- left_next: float32 [16, 4, 4, 512, 512], P('dp', 'mp', 'pre')
- right_next: float32 [16, 4, 4, 512, 512], P('dp', 'mp', 'pre')
- update: float32 [16, 4, 4, 512, 512], P('dp', 'mp', 'pre')
Inputs may be any that keep to these rules, and one draw needn't show every extreme that they name: `left_stat`: every block [k, m, p] is symmetric and positive definite. `right_stat`: every block [k, m, p] is symmetric and positive definite.
All inputs are finite; a program needn't handle non-finite values.
Results may differ from a plain program's by a relative error of at most 0.001.
Values may be sent and summed in bfloat16 or wider, within the bound.
A program may use at most 128 MiB of HBM per device.

v0:
```python
import jax
import jax.numpy as jnp
from jax import lax
from jax.sharding import PartitionSpec as P

D = 4096
FF = 16384


DECAY_RATE = 0.9
EXACT_PRECISION = lax.Precision.HIGHEST


def batch_product(former, latter):
    return jnp.einsum(
        "nij,njk->nik",
        former,
        latter,
        precision=EXACT_PRECISION,
        preferred_element_type=jnp.float32,
    )


def inverse_root(statistic):
    block_size = statistic.shape[-1]
    identity = jnp.eye(block_size, dtype=jnp.float32)
    frobenius = jnp.sqrt(jnp.sum(statistic * statistic, axis=(1, 2), keepdims=True))
    scaling = 2.5 / frobenius
    matrix = scaling * statistic
    factor = (5.0 * identity - matrix) / 4.0
    root_now = scaling**0.25 * factor
    square = batch_product(factor, factor)
    matrix = batch_product(batch_product(square, square), matrix)
    factor = (5.0 * identity - matrix) / 4.0
    root_now = batch_product(root_now, factor)
    return root_now


def on_device(activations, cotangent, weight_blocks, left_stat, right_stat):
    tokens_here = activations.shape[0]
    hidden_shard = activations.shape[1]
    width_shard = cotangent.shape[1]
    block_size = weight_blocks.shape[-1]
    row_tiles = hidden_shard // block_size
    column_tiles = width_shard // block_size
    owned_block_count = weight_blocks.shape[0]
    groups = lax.axis_size("dp")
    total_tokens = tokens_here * groups
    activation_tiles = activations.reshape(tokens_here, row_tiles, block_size)
    cotangent_tiles = cotangent.reshape(tokens_here, column_tiles, block_size)
    inner_position = jnp.arange(lax.axis_size("dp") * owned_block_count, dtype=jnp.int32)
    activation_picked = jnp.take(activation_tiles, inner_position // column_tiles, axis=1)
    cotangent_picked = jnp.take(cotangent_tiles, inner_position % column_tiles, axis=1)
    summed = lax.psum_scatter(
        jnp.einsum(
            "tna,tnb->nab", activation_picked, cotangent_picked, preferred_element_type=jnp.float32
        ),
        "dp",
        scatter_dimension=0,
        tiled=True,
    )
    grad_block = summed / total_tokens
    segment = lax.all_gather(weight_blocks, "dp", axis=0, tiled=True)
    segment_count = segment.shape[0]
    inner_position = jnp.arange(segment_count, dtype=jnp.int32)
    row_position = inner_position // column_tiles
    column_position = inner_position % column_tiles
    chosen = jnp.zeros((tokens_here, segment_count, block_size), cotangent.dtype)
    for column in range(column_tiles):
        chosen = jnp.where(
            (column_position == column)[None, :, None],
            cotangent_tiles[:, column : column + 1, :],
            chosen,
        )
    tile_products = jnp.einsum(
        "tnd,nfd->tnf",
        chosen,
        segment.reshape(segment_count, block_size, block_size),
        preferred_element_type=jnp.float32,
    )
    block_placing = (
        row_position[:, None] == jnp.arange(row_tiles, dtype=jnp.int32)[None, :]
    ).astype(jnp.float32)
    partial_result_value = jnp.einsum(
        "lpq,pb->lbq", tile_products, block_placing, precision=EXACT_PRECISION
    )
    input_grad = lax.psum_scatter(
        partial_result_value.reshape(tokens_here, hidden_shard),
        "pre",
        scatter_dimension=1,
        tiled=True,
    ).astype(jnp.bfloat16)
    left_old = left_stat.reshape(owned_block_count, block_size, block_size)
    right_old = right_stat.reshape(owned_block_count, block_size, block_size)
    grad_turned = jnp.swapaxes(grad_block, 1, 2)
    left_next = DECAY_RATE * left_old + (1.0 - DECAY_RATE) * batch_product(grad_block, grad_turned)
    right_next = DECAY_RATE * right_old + (1.0 - DECAY_RATE) * batch_product(
        grad_turned, grad_block
    )
    left_root = inverse_root(left_next)
    right_root = inverse_root(right_next)
    raw_update = batch_product(batch_product(left_root, grad_block), right_root)
    square_sum = lax.psum(jnp.sum(raw_update * raw_update), ("dp", "mp", "pre"))
    update = raw_update / jnp.sqrt(square_sum / (FF * D) + 1e-06)
    shape_out = left_stat.shape
    return (
        input_grad,
        left_next.reshape(shape_out),
        right_next.reshape(shape_out),
        update.reshape(shape_out),
    )


def solution(mesh):
    in_specs = (
        P("dp", "mp"),
        P("dp", "pre"),
        P("dp", "mp", "pre", None, None),
        P("dp", "mp", "pre", None, None),
        P("dp", "mp", "pre", None, None),
    )
    out_specs = (
        P("dp", ("mp", "pre")),
        P("dp", "mp", "pre", None, None),
        P("dp", "mp", "pre", None, None),
        P("dp", "mp", "pre", None, None),
    )
    return jax.shard_map(
        on_device, mesh=mesh, in_specs=in_specs, out_specs=out_specs, check_vma=False
    )
```

profile of v0, /device:TPU:32, one launch (start us, length us, event | category | flops | bytes accessed | tf_op | source)
XLA Modules:
  0.0 533.1 jit_solution(16010448111516372930)
XLA Ops:
  7.2 0.0 all-gather.2.cloned.1.call-start
  7.2 0.7 all-gather.2.cloned.1.call-update
  7.9 0.0 reduce-scatter.3.cloned.1.call-start
  7.9 1.2 copy.20
  9.2 0.1 copy.21
  9.4 0.1 copy.22
  9.6 119.5 %all-gather.2.cloned.1.call-done = bf16[16,1,1,512,512]{4,3,2,1,0:T(8,128)(2,1)} async-done(((bf16[1,1,1,512,512]{4,3,2,1,0:T(8,128)(2,1)}), bf16[16,1,1,512,512]{4,3,2,1,0:T(8,128)(2,1)}) %all-gather.2.cloned.1.call-update) | async-done | bytes 8388624 | tf_op jit(solution)/shard_map/all_gather | solution.py:63
  129.0 5.8 %fusion.15 = f32[256,16,512]{2,0,1:T(8,128)S(1)} fusion(bf16[16,1,1,512,512]{4,3,2,1,0:T(8,128)(2,1)} %all-gather.2.cloned.1.call-done, pred[16]{0:T(512)(128)(4,1)S(1)} %get-tuple-element.12, pred[16]{0:T(512)(128)(4,1)S(1)} %get-tuple-element.13, bf16[256,512]{1,0:T(8,128)(2,1)S(1)} %bitcast.65, bf16[256,512]{1,0:T(8,128)(2,1)S(1)} %bitcast.64), kind=kOutput, calls=%fused_computation.17 | convolution fusion | flops 2151677952 | bytes 17301536 | tf_op jit(solution)/shard_map/tnd,nfd->tnf/dot_general | solution.py:75
  134.8 7.9 %fusion.2 = f32[8,256,512]{2,0,1:T(8,128)S(1)} fusion(f32[256,16,512]{2,0,1:T(8,128)S(1)} %fusion.15, s32[16]{0:T(128)S(1)} %and_select_fusion.3), kind=kOutput, calls=%fused_computation.4 | convolution fusion | flops 201326720 | bytes 12582976 | tf_op jit(solution)/shard_map/lpq,pb->lbq/dot_general | solution.py:84
  142.7 16.7 %copy.29 = f32[32,8,8,512]{3,1,2,0:T(8,128)} copy(f32[32,8,8,512]{3,2,1,0:T(8,128)S(1)} %bitcast.58) | data formatting | bytes 8388608
  159.4 0.0 copy-start.4
  159.4 0.0 reduce-scatter.3.cloned.1.call-update
  159.4 0.0 reduce-scatter.5.cloned.1.call-start
  159.4 0.2 copy.26
  159.7 1.3 copy-done.4
  161.0 2.4 copy.24
  163.4 2.9 copy.25
  166.3 2.8 gather_fusion
  169.1 2.8 gather_fusion.1
  171.8 11.8 %fusion.4 = f32[16,512,512]{2,1,0:T(8,128)} fusion(bf16[16,256,512]{2,1,0:T(8,128)(2,1)} %gather_fusion.1, bf16[16,256,512]{2,1,0:T(8,128)(2,1)} %gather_fusion, pred[16]{0:T(512)(128)(4,1)S(1)} %get-tuple-element.14, pred[16]{0:T(512)(128)(4,1)S(1)} %get-tuple-element.15), kind=kOutput, calls=%fused_computation.6 | convolution fusion | flops 2151677952 | bytes 25165856 | tf_op jit(solution)/shard_map/tna,tnb->nab/dot_general | solution.py:55
  183.6 0.0 copy-start.5
  183.6 0.0 reduce-scatter.5.cloned.1.call-update
  183.7 21.1 %reduce-scatter.3.cloned.1.call-done = f32[256,1024]{1,0:T(8,128)} async-done(((f32[256,4096]{1,0:T(8,128)}), f32[256,1024]{1,0:T(8,128)}) %reduce-scatter.3.cloned.1.call-update) | async-done | bytes 1048592 | tf_op jit(solution)/shard_map/reduce_scatter | solution.py:87
  204.7 2.1 convert_element_type.2
  206.8 209.1 %reduce-scatter.5.cloned.1.call-done = f32[1,512,512]{2,1,0:T(8,128)} async-done(((f32[16,512,512]{2,1,0:T(8,128)}), f32[1,512,512]{2,1,0:T(8,128)}) %reduce-scatter.5.cloned.1.call-update) | async-done | bytes 1048592 | tf_op jit(solution)/shard_map/reduce_scatter | solution.py:54
  415.9 0.0 copy-done.5
  415.9 4.2 multiply_reduce_fusion.1
  420.2 0.0 copy-start.1
  420.9 0.0 copy-start
  420.9 0.0 copy-start.6
  420.9 2.0 fusion.32
  422.9 1.8 fusion.88
  424.8 2.8 fusion.27
  427.6 0.0 copy-done
  427.6 0.0 copy-done.6
  427.6 2.9 multiply_reduce_fusion.2
  430.5 0.0 copy-start.2
  431.2 0.0 copy-start.3
  431.2 2.0 fusion.36
  433.2 1.8 fusion.87
  435.0 1.9 fusion.26
  436.9 0.0 copy-done.1
  436.9 0.0 copy-done.3
  436.9 2.0 fusion.34
  438.9 0.0 copy-done.2
  438.9 2.0 fusion.38
  440.9 1.9 fusion.28
  442.8 2.6 multiply_reduce_fusion
  445.3 79.1 %psum.7 = f32[]{:T(128)} all-reduce(f32[]{:T(128)} %get-tuple-element.10), channel_id=1, replica_groups=mesh['dp'=16,'mp'=4,'pre'=4] {'dp','mp','pre'}, use_global_device_ids=true, to_apply=%region_5.6 | all-reduce | flops 1 | bytes 8 | tf_op jit(solution)/shard_map/psum | solution.py:103
  525.1 1.1 divide_bitcast_fusion
  (8 shorter events, 0.1 us)
Async XLA Ops:
  7.2 121.8 %all-gather.2.cloned.1.call-start = ((), (), s32[]{:S(2)}) async-start(), calls=%async_computation.2 | async-start | bytes 8912896 | tf_op jit(solution)/shard_map/all_gather | solution.py:63
  7.9 196.8 %reduce-scatter.3.cloned.1.call-start = ((), (), s32[]{:S(2)}) async-start(), calls=%async_computation.3 | async-start | bytes 5242880 | tf_op jit(solution)/shard_map/reduce_scatter | solution.py:87
  159.4 1.6 copy-start.4
  159.4 256.5 %reduce-scatter.5.cloned.1.call-start = ((), (), s32[]{:S(2)}) async-start(), calls=%async_computation.4 | async-start | bytes 17825792 | tf_op jit(solution)/shard_map/reduce_scatter | solution.py:54
  183.6 232.3 %copy-start.5 = (f32[1,1,1,512,512]{4,3,2,1,0:T(8,128)S(1)}, f32[1,1,1,512,512]{4,3,2,1,0:T(8,128)}, u32[]{:S(2)}) copy-start(f32[1,1,1,512,512]{4,3,2,1,0:T(8,128)} %param.9) | copy-start | bytes 3145732
  420.2 16.7 %copy-start.1 = (f32[512,512]{1,0:T(8,128)}, f32[512,512]{1,0:T(8,128)S(1)}, u32[]{:S(2)}) copy-start(f32[512,512]{1,0:T(8,128)S(1)} %get-tuple-element.9) | copy-start | bytes 3145732
  420.9 6.7 %copy-start = (f32[1,512,512]{2,1,0:T(8,128)S(1)}, f32[1,512,512]{2,1,0:T(8,128)}, u32[]{:S(2)}) copy-start(f32[1,512,512]{2,1,0:T(8,128)} %reduce-scatter.5.cloned.1.call-done) | copy-start | bytes 3145732
  420.9 6.7 %copy-start.6 = (f32[1,1,1,512,512]{4,3,2,1,0:T(8,128)S(1)}, f32[1,1,1,512,512]{4,3,2,1,0:T(8,128)}, u32[]{:S(2)}) copy-start(f32[1,1,1,512,512]{4,3,2,1,0:T(8,128)} %param.8) | copy-start | bytes 3145732
  430.5 8.4 %copy-start.2 = (f32[512,512]{1,0:T(8,128)}, f32[512,512]{1,0:T(8,128)S(1)}, u32[]{:S(2)}) copy-start(f32[512,512]{1,0:T(8,128)S(1)} %get-tuple-element.7) | copy-start | bytes 3145732
  431.2 5.7 %copy-start.3 = (f32[512,512]{1,0:T(8,128)S(1)}, f32[512,512]{1,0:T(8,128)}, u32[]{:S(2)}) copy-start(f32[512,512]{1,0:T(8,128)} %fusion.27) | copy-start | bytes 3145732
Sparse Core Ops, SparseCore 0:
  10.4 118.5 all-gather.1
  159.5 45.1 reduce-scatter.2
  208.9 207.0 reduce-scatter.4
where the time goes:
time: 543 us; the launch traced here: 533 us
  waiting for transfers between devices  350 us (64%)
  blocking collectives  79.1 us (15%)
  matrix products  53.2 us (10%)
  local copies, waits for them, and re-layouts  30.6 us (6%)
  between operations  16.5 us (3%)
    reduce_scatter x1, waiting for transfers between devices, on_device(): lax.psum_scatter(jnp.einsum('tna,tnb->nab', activation_picked, cotangent_...  209 us
    all_gather x1, waiting for transfers between devices, on_device(): segment = lax.all_gather(weight_blocks, 'dp', axis=0, tiled=True)  119 us
    psum x1, blocking collectives, on_device(): square_sum = lax.psum(jnp.sum(raw_update * raw_update), ('dp', 'mp', 'pre'))  79.1 us
    dot_general x12, matrix products, batch_product(): jnp.einsum('nij,njk->nik', former, latter, precision=EXACT_PRECISION, pre...  27.8 us
    unnamed x17, local copies, waits for them, and re-layouts  21.7 us
    reduce_scatter x1, waiting for transfers between devices, on_device(): lax.psum_scatter(partial_result_value.reshape(tokens_here, hidden_shard),...  21.1 us
    dot_general x1, matrix products, on_device(): jnp.einsum('tna,tnb->nab', activation_picked, cotangent_picked, preferred...  11.8 us
  transfers between devices with their start and end apart: 3, of which 3 were waited for; matrix products, arithmetic and copies ran while one was open for 5% of the time, Pallas kernels for 0%

commit v1 on v0

v1 whole, which is shorter than its diff:
```python
import jax
import jax.numpy as jnp
from jax import lax
from jax.experimental import pallas as pl
from jax.experimental.pallas import tpu as pltpu
from jax.sharding import PartitionSpec as P

D = 4096
FF = 16384
TOKENS = 4096
BLOCK = 512
NX, NY, NZ = 4, 4, 8

DECAY_RATE = 0.9
MESH = pl.DeviceIdType.MESH
DMA = pltpu.SemaphoreType.DMA
HIGH = lax.Precision.HIGH


def gather_kernel(
    act, cot, wblk,
    ig_out, grad_out,
    ACT, OUTB, COT, CIG, WB, ACC, OB,
    loc_sem, a1_s, a1_r, a1o_s, a1o_r, tz_s, tz_r, sw_s, sw_r,
    b1_s, b1_r, ring_s, ring_r, c1_s, c1_r, w_s, w_r, ws_s, ws_r, o_s, o_r,
):
    dp = lax.axis_index("dp")
    y = lax.axis_index("mp")
    pre = lax.axis_index("pre")
    x = lax.div(dp, 4)
    zh = lax.rem(dp, 4)
    zl = lax.div(pre, 2)
    c = lax.rem(pre, 2)
    oc = 1 - c
    z = zh * 2 + zl
    grp = lax.div(z, 4)
    g = lax.rem(z, 4)
    side = lax.div(g, 2)
    inner = lax.rem(lax.div(g + 1, 2), 2)
    d = 1 - 2 * side
    so, sn, sf, se = 1 + side, 3 * side, 2 - side, 3 - 3 * side
    hpar = lax.rem(zh, 2)

    def dev(xx, yy, zz, cc):
        return {
            "dp": xx * 4 + lax.div(zz, 2),
            "mp": yy,
            "pre": lax.rem(zz, 2) * 2 + cc,
        }

    def xp(k):
        return lax.rem(x + k + 4, 4)

    def yp(k):
        return lax.rem(y + k + 4, 4)

    def zp(k):
        return lax.rem(z + k + 8, 8)

    def zp_d(sign):
        return lax.rem(z + sign * d + 8, 8)

    other = dev(x, y, z, oc)

    barrier = pltpu.get_barrier_semaphore()
    count = 0

    def greet(device):
        pl.semaphore_signal(barrier, inc=1, device_id=device, device_id_type=MESH)

    for k in range(4):
        for m in range(4):
            if k or m:
                greet({"dp": xp(k) * 4 + zh, "mp": y, "pre": lax.rem(pre + m, 4)})
                count += 1
    for k in range(1, 4):
        greet(dev(x, yp(k), z, c))
        count += 1
    greet(dev(x, y, lax.rem(z + 2 * zl - 1 + 8, 8), c))
    greet(dev(x, y, zp(2), c))
    greet(dev(x, y, zp(-2), c))
    greet(dev(x, y, zp(4), c))
    count += 4
    pl.semaphore_wait(barrier, count)

    sends = []

    def remote(src, dst, ssem, rsem, device, when=None):
        cp = pltpu.make_async_remote_copy(
            src_ref=src, dst_ref=dst, send_sem=ssem, recv_sem=rsem,
            device_id=device, device_id_type=MESH,
        )
        if when is None:
            cp.start()
        else:
            @pl.when(when)
            def _():
                cp.start()
        sends.append((when, cp))

    def arrived(dst, rsem):
        pltpu.make_async_copy(dst, dst, rsem).wait()

    is_inner = inner == 1
    is_outer = inner == 0

    def act_src(xx, gg):
        return act.at[
            pl.ds(pl.multiple_of(c * 128, 128), 128),
            pl.ds(pl.multiple_of(xx * 1024 + gg * 512, 512), 512),
        ]

    rel = (0, -1, 1, 2)
    xs = [xp(r) for r in rel]
    cot_piece = lambda half: cot.at[
        pl.ds(pl.multiple_of(y * 64, 64), 64),
        pl.ds(pl.multiple_of(half * 512, 512), 512),
    ]
    ypair = lax.div(y, 2)
    ylow = lax.rem(y, 2)
    cot_slot = lambda zz: COT.at[zz, ypair, x, ylow]
    pltpu.make_async_copy(cot_piece(hpar), cot_slot(zh), loc_sem.at[0]).start()
    remote(cot_piece(hpar), cot_slot(zh), b1_s.at[0], b1_r.at[0], dev(x, y, zp(4), c))
    remote(cot_piece(1 - hpar), cot_slot(zh), b1_s.at[1], b1_r.at[1], dev(x, y, zp(2), c))
    remote(cot_piece(1 - hpar), cot_slot(zh), b1_s.at[2], b1_r.at[2], dev(x, y, zp(-2), c))
    pltpu.make_async_copy(act_src(x, grp), ACT.at[so, c, x], loc_sem.at[1]).start()

    @pl.when(is_outer)
    def _():
        pltpu.make_async_copy(act_src(x, 1 - grp), OUTB.at[x], loc_sem.at[2]).start()

    for k, step in ((1, 1), (2, -1), (3, 2)):
        to = xp(step)
        remote(act_src(to, 1 - grp), OUTB.at[x], a1o_s.at[k], a1o_r.at[k],
               dev(to, y, z, c), when=is_outer)
        remote(act_src(to, grp), ACT.at[so, c, x], a1_s.at[k], a1_r.at[k], dev(to, y, z, c))
    cig_src = lambda q: cot.at[pl.ds(pl.multiple_of(q * 64, 64), 64), :]
    pltpu.make_async_copy(cig_src(pre), CIG.at[pre, x], loc_sem.at[3]).start()
    for k in range(1, 4):
        q = lax.rem(pre + k, 4)
        remote(cig_src(q), CIG.at[pre, x], c1_s.at[k], c1_r.at[k],
               {"dp": dp, "mp": y, "pre": q})
    pltpu.make_async_copy(wblk, WB.at[z, c], loc_sem.at[4]).start()
    remote(wblk, WB.at[z, c], ws_s.at[0], ws_r.at[0], other)

    def ring_start(base, unit, my, to_next, to_prev):
        remote(unit(my, 0, 2), unit(my, 0, 2), ring_s.at[base], ring_r.at[base], to_next)
        remote(unit(my, 0, 2), unit(my, 0, 2), ring_s.at[base + 1], ring_r.at[base + 1], to_prev)

    def ring_forward(base, unit, prv, nxt, to_next, to_prev):
        arrived(unit(prv, 0, 2), ring_r.at[base])
        remote(unit(prv, 0, 1), unit(prv, 0, 1), ring_s.at[base + 2], ring_r.at[base + 2], to_next)
        arrived(unit(nxt, 0, 2), ring_r.at[base + 1])
        remote(unit(nxt, 1, 1), unit(nxt, 1, 1), ring_s.at[base + 3], ring_r.at[base + 3], to_prev)

    def ring_end(base, unit, far):
        arrived(unit(far, 0, 1), ring_r.at[base + 2])
        arrived(unit(far, 1, 1), ring_r.at[base + 3])

    xnext, xprev = dev(xp(1), y, z, c), dev(xp(-1), y, z, c)
    ynext, yprev = dev(x, yp(1), z, c), dev(x, yp(-1), z, c)
    u1a = lambda i, lo, n: COT.at[pl.ds(lo, n), ypair, i, ylow]
    u2a = lambda i, lo, n: COT.at[pl.ds(2 + lo, n), lax.div(i, 2), x, lax.rem(i, 2)]
    u1b = lambda i, lo, n: COT.at[pl.ds(lo, n), lax.div(i, 2), :, lax.rem(i, 2)]
    u2b = lambda i, lo, n: COT.at[pl.ds(2 + lo, n), :, i]
    uc = lambda i, lo, n: CIG.at[pl.ds(2 * lo, 2 * n), i]
    xargs = (xp(-1), xp(1), xnext, xprev)
    yargs = (yp(-1), yp(1), ynext, yprev)

    inward = dev(x, y, zp_d(1), c)
    outward = dev(x, y, zp_d(-1), c)
    kind_n = 2 * inner

    def swap(kind, k, slot):
        piece = ACT.at[slot, c, xs[k]]
        remote(piece, piece, sw_s.at[kind, k], sw_r.at[kind, k], other)

    def own(k):
        piece = ACT.at[so, c, xs[k]]
        if k == 0:
            pltpu.make_async_copy(act_src(x, grp), piece, loc_sem.at[1]).wait()

            @pl.when(is_outer)
            def _():
                pltpu.make_async_copy(act_src(x, 1 - grp), OUTB.at[x], loc_sem.at[2]).wait()
        else:
            @pl.when(is_outer)
            def _():
                arrived(OUTB.at[xs[k]], a1o_r.at[k])

        remote(OUTB.at[xs[k]], ACT.at[3 - sn, c, xs[k]],
               tz_s.at[0, k], tz_r.at[0, k], outward, when=is_outer)
        if k:
            arrived(piece, a1_r.at[k])
        remote(piece, piece, tz_s.at[1, k], tz_r.at[1, k], inward, when=is_inner)
        swap(3, k, so)

    def near(k):
        piece = ACT.at[sn, c, xs[k]]
        arrived(piece, tz_r.at[0, k])
        remote(piece, piece, tz_s.at[2, k], tz_r.at[kind_n, k], inward)
        swap(0, k, sn)

    def far(k):
        piece = ACT.at[sf, c, xs[k]]
        arrived(piece, tz_r.at[1, k])
        remote(piece, piece, tz_s.at[3, k], tz_r.at[1, k], outward, when=is_inner)
        swap(1, k, sf)

    def end(k):
        piece = ACT.at[se, c, xs[k]]
        arrived(piece, tz_r.at[2, k])
        remote(piece, piece, tz_s.at[4, k], tz_r.at[2, k], outward, when=is_inner)
        swap(2, k, se)

    own(0)
    pltpu.make_async_copy(cot_piece(hpar), cot_slot(zh), loc_sem.at[0]).wait()
    arrived(cot_slot(lax.rem(zh + 2, 4)), b1_r.at[0])
    arrived(cot_slot(lax.rem(zh + 3, 4)), b1_r.at[1])
    arrived(cot_slot(lax.rem(zh + 1, 4)), b1_r.at[2])
    ring_start(0, u1a, x, xnext, xprev)
    ring_start(4, u2a, y, ynext, yprev)
    own(1)
    own(2)
    near(0)
    ring_forward(0, u1a, *xargs)
    ring_forward(4, u2a, *yargs)
    far(0)
    near(1)
    ring_end(0, u1a, xp(2))
    ring_end(4, u2a, yp(2))
    ring_start(8, u1b, y, ynext, yprev)
    ring_start(12, u2b, x, xnext, xprev)
    own(3)
    near(2)
    far(1)
    end(0)
    near(3)
    far(2)
    end(1)
    far(3)
    end(2)
    end(3)
    pltpu.make_async_copy(wblk, WB.at[z, c], loc_sem.at[4]).wait()
    znext, zprev = dev(x, y, zp(1), c), dev(x, y, zp(-1), c)
    wpart = lambda zz, hf: WB.at[zz, c, pl.ds(hf * 256, 256)]

    def w_send(way, t, hf):
        zz = zp(-(t - 1)) if way == 0 else zp(t - 1)
        remote(wpart(zz, hf), wpart(zz, hf), w_s.at[way, t, hf], w_r.at[way, t, hf],
               znext if way == 0 else zprev)

    for hf in range(2):
        for way in range(2):
            w_send(way, 1, hf)
    ring_forward(8, u1b, *yargs)
    ring_forward(12, u2b, *xargs)
    ring_end(8, u1b, yp(2))
    ring_end(12, u2b, xp(2))
    pltpu.make_async_copy(cig_src(pre), CIG.at[pre, x], loc_sem.at[3]).wait()
    for k in range(1, 4):
        arrived(CIG.at[lax.rem(pre + 4 - k, 4), x], c1_r.at[k])
    ring_start(16, uc, x, xnext, xprev)
    for kind, slot in ((3, so), (0, sn), (1, sf), (2, se)):
        for k in range(4):
            arrived(ACT.at[slot, oc, xs[k]], sw_r.at[kind, k])

    grad_out[...] = jnp.zeros((BLOCK, BLOCK), jnp.float32)

    @pl.loop(0, 8)
    def _(i):
        s = lax.div(i, 2)
        cc = lax.rem(i, 2)
        shard = lax.rem(2 * grp + 3 + s, 4)
        a = ACT[s, cc].reshape(BLOCK, BLOCK)
        b = COT[shard, cc].reshape(BLOCK, BLOCK)
        grad_out[...] += lax.dot_general(
            a, b, (((0,), (0,)), ((), ())), preferred_element_type=jnp.float32
        )

    grad_out[...] = grad_out[...] * (1.0 / TOKENS)

    ACC[...] = jnp.zeros_like(ACC)

    def w_swap(way, t, hf):
        zz = zp(-t) if way == 0 else zp(t)
        remote(wpart(zz, hf), wpart(zz, hf), ws_s.at[1 + (way * 5 + t) * 2 + hf],
               ws_r.at[1 + (way * 5 + t) * 2 + hf], other)

    def ig_part(zz, cc, r0, rows):
        p = lax.rem(zz, 2) * 2 + cc
        h = lax.rem(lax.div(zz, 2), 2)
        a = CIG[p, :, :, pl.ds(pl.multiple_of(h * 512, 512), 512)].reshape(256, 512)
        w = WB[zz, cc, pl.ds(r0, rows)]
        out = lax.dot_general(a, w, (((1,), (1,)), ((), ())), preferred_element_type=jnp.float32)
        ACC[lax.div(zz, 4), :, pl.ds(r0, rows)] += out

    def w_arrive(way, t, hf):
        zz = zp(-t) if way == 0 else zp(t)
        arrived(wpart(zz, hf), w_r.at[way, t, hf])
        if t < 3 or (t == 3 and hf == way):
            w_send(way, t + 1, hf)
        w_swap(way, t, hf)

    def other_half(way, t, hf):
        zz = zp(-t) if way == 0 else zp(t)
        arrived(WB.at[zz, oc, pl.ds(hf * 256, 256)], ws_r.at[1 + (way * 5 + t) * 2 + hf])

    ring_forward(16, uc, *xargs)
    for hf in range(2):
        for way in range(2):
            w_arrive(way, 1, hf)
    ring_end(16, uc, xp(2))
    arrived(WB.at[z, oc], ws_r.at[0])
    ig_part(z, c, 0, 512)
    ig_part(z, oc, 0, 512)
    for t in range(2, 5):
        for hf in range(2):
            for way in range(2):
                if t < 4 or hf == way:
                    w_arrive(way, t, hf)
        for way in range(2):
            zz = zp(-(t - 1)) if way == 0 else zp(t - 1)
            for hf in range(2):
                other_half(way, t - 1, hf)
            ig_part(zz, c, 0, 512)
            ig_part(zz, oc, 0, 512)
    z4 = zp(4)
    for way in range(2):
        other_half(way, 4, way)
    ig_part(z4, c, 0, 512)
    ig_part(z4, oc, 0, 512)

    for j in range(2):
        OB[:, :, pl.ds(j * 512, 512)] = ACC[j].reshape(4, 64, 512).astype(jnp.bfloat16)
    sub = zl * 2 + c
    z_to = zh * 2 + lax.div(x, 2)
    c_to = lax.rem(x, 2)
    rows = ig_out.at[pl.ds(pl.multiple_of(sub * 64, 64), 64), :]
    mine = pre == x
    for k in range(4):
        xt = xs[k]
        dst = dev(xt, y, z_to, c_to)
        if k == 0:
            remote(OB.at[xt], rows, o_s.at[k], o_r.at[sub], dst, when=jnp.logical_not(mine))

            @pl.when(mine)
            def _():
                cp = pltpu.make_async_copy(OB.at[x], rows, loc_sem.at[5])
                cp.start()
                cp.wait()
        else:
            remote(OB.at[xt], rows, o_s.at[k], o_r.at[sub], dst)
    for q in range(4):
        piece = ig_out.at[pl.ds(q * 64, 64), :]

        @pl.when(jnp.logical_not(jnp.logical_and(mine, sub == q)))
        def _():
            arrived(piece, o_r.at[q])

    for when, cp in sends:
        if when is None:
            cp.wait_send()
        else:
            pl.when(when)(cp.wait_send)


def gather_call(act, cot, wblk):
    any_spec = pl.BlockSpec(memory_space=pl.ANY)
    vmem = pl.BlockSpec(memory_space=pltpu.VMEM)
    bf = jnp.bfloat16
    return pl.pallas_call(
        gather_kernel,
        out_shape=(
            jax.ShapeDtypeStruct((256, 1024), bf),
            jax.ShapeDtypeStruct((BLOCK, BLOCK), jnp.float32),
        ),
        in_specs=[any_spec] * 3,
        out_specs=(any_spec, vmem),
        scratch_shapes=[
            pltpu.VMEM((4, 2, 4, 128, 512), bf),
            pltpu.VMEM((4, 128, 512), bf),
            pltpu.VMEM((4, 2, 4, 2, 64, 512), bf),
            pltpu.VMEM((4, 4, 64, 1024), bf),
            pltpu.VMEM((8, 2, 512, 512), bf),
            pltpu.VMEM((2, 256, 512), jnp.float32),
            pltpu.VMEM((4, 64, 1024), bf),
            DMA((6,)), DMA((4,)), DMA((4,)), DMA((4,)), DMA((4,)),
            DMA((5, 4)), DMA((3, 4)), DMA((4, 4)), DMA((4, 4)),
            DMA((3,)), DMA((3,)), DMA((20,)), DMA((20,)), DMA((4,)), DMA((4,)),
            DMA((2, 5, 2)), DMA((2, 5, 2)), DMA((21,)), DMA((21,)), DMA((4,)), DMA((4,)),
        ],
        compiler_params=pltpu.CompilerParams(
            collective_id=0, has_side_effects=True, vmem_limit_bytes=48 * 1024 * 1024
        ),
        name="gather_products",
    )(act, cot, wblk)


def product(former, latter):
    return jnp.dot(former, latter, precision=HIGH, preferred_element_type=jnp.float32)


def inverse_root(statistic):
    identity = jnp.eye(BLOCK, dtype=jnp.float32)
    frobenius = jnp.sqrt(jnp.sum(statistic * statistic))
    scaling = 2.5 / frobenius
    matrix = scaling * statistic
    factor = (5.0 * identity - matrix) / 4.0
    square = product(factor, factor)
    matrix = product(product(square, square), matrix)
    later = (5.0 * identity - matrix) / 4.0
    return product(scaling**0.25 * factor, later)


def on_device(activations, cotangent, weight_blocks, left_stat, right_stat):
    input_grad, grad = gather_call(
        activations, cotangent, weight_blocks.reshape(BLOCK, BLOCK)
    )
    left_old = left_stat.reshape(BLOCK, BLOCK)
    right_old = right_stat.reshape(BLOCK, BLOCK)
    left_next = DECAY_RATE * left_old + (1.0 - DECAY_RATE) * product(grad, grad.T)
    right_next = DECAY_RATE * right_old + (1.0 - DECAY_RATE) * product(grad.T, grad)
    raw_update = product(product(inverse_root(left_next), grad), inverse_root(right_next))
    square_sum = lax.psum(jnp.sum(raw_update * raw_update), ("dp", "mp", "pre"))
    update = raw_update / jnp.sqrt(square_sum / (FF * D) + 1e-06)
    shape_out = left_stat.shape
    return (
        input_grad,
        left_next.reshape(shape_out),
        right_next.reshape(shape_out),
        update.reshape(shape_out),
    )


def solution(mesh):
    block = P("dp", "mp", "pre", None, None)
    return jax.shard_map(
        on_device,
        mesh=mesh,
        in_specs=(P("dp", "mp"), P("dp", "pre"), block, block, block),
        out_specs=(P("dp", ("mp", "pre")), block, block, block),
        check_vma=False,
    )
```

time: 543 us -> 232 us (0.43); the launches traced: 533 us -> 230 us
  waiting for transfers between devices: 350 us -> 0 us
  Pallas kernels: 0 us -> 126 us
  matrix products: 53.2 us -> 20.9 us
  local copies, waits for them, and re-layouts: 30.6 us -> 4.48 us
  between operations: 16.5 us -> 2.85 us
    reduce_scatter x2 -> x0, waiting for transfers between devices: 230 us -> none  [the longest x1 209 us: on_device(): lax.psum_scatter(jnp.einsum('tna,tnb->nab', activation_picked, cotangent_...]
    pallas_call x0 -> x1, Pallas kernels: none -> 126 us  [gather_call(): pl.pallas_call(gather_kernel, out_shape=(jax.ShapeDtypeStruct((256, 1024)...]
    all_gather x1 -> x0, waiting for transfers between devices: 119 us -> none  [on_device(): segment = lax.all_gather(weight_blocks, 'dp', axis=0, tiled=True)]
    dot_general x15 -> x12, matrix products: 53.2 us -> 20.9 us  [product(): jnp.dot(former, latter, precision=HIGH, preferred_element_type=jnp.float32)]
    unnamed x17, local copies, waits for them, and re-layouts: 21.7 us -> 4.48 us
    gather x2 -> x0, local copies, waits for them, and re-layouts: 5.53 us -> none  [the longest x1 2.78 us: on_device(): jnp.take(cotangent_tiles, inner_position % column_tiles, axis=1)]
  transfers between devices with their start and end apart: 3 -> 0, of which waited for: 3 -> 0; matrix products, arithmetic and copies ran while one was open for 5% -> 0% of each run, Pallas kernels for 0% -> 0%
where the time goes in v1:
time: 232 us; the launch traced here: 230 us
  Pallas kernels  126 us (54%)
  blocking collectives  74.6 us (32%)
  matrix products  20.9 us (9%)
  local copies, waits for them, and re-layouts  4.48 us (2%)
  between operations  2.85 us (1%)
    pallas_call x1, Pallas kernels, gather_call(): pl.pallas_call(gather_kernel, out_shape=(jax.ShapeDtypeStruct((256, 1024)...  126 us
    psum x1, blocking collectives, on_device(): square_sum = lax.psum(jnp.sum(raw_update * raw_update), ('dp', 'mp', 'pre'))  74.6 us
    dot_general x12, matrix products, product(): jnp.dot(former, latter, precision=HIGH, preferred_element_type=jnp.float32)  20.9 us

profile of v1, /device:TPU:32, one launch (start us, length us, event | category | flops | bytes accessed | tf_op | source)
XLA Modules:
  0.0 230.2 jit_solution(6492114567467456681)
XLA Ops:
  0.6 0.0 copy-start
  0.6 1.6 copy-done
  2.2 0.0 copy-start.1
  2.2 1.0 copy-done.1
  3.3 0.0 copy-start.2
  3.3 1.0 copy-done.2
  4.3 0.0 copy-start.6
  4.3 126.3 %gather_products.1 = (bf16[256,1024]{1,0:T(8,128)(2,1)S(1)}, f32[512,512]{1,0:T(8,128)S(1)}) custom-call(bf16[256,4096]{1,0:T(8,128)(2,1)S(1)} %copy-done, bf16[256,1024]{1,0:T(8,128)(2,1)S(1)} %copy-done.1, bf16[512,512]{1,0:T(8,128)(2,1)S(1)} %bitcast.25), custom_call_target="tpu_custom_call" | custom-call | tf_op jit(solution)/shard_map/gather_products/pallas_call | solution.py:372
  130.7 0.0 copy-done.6
  130.7 0.0 copy-start.7
  130.7 1.8 multiply_reduce_fusion.2
  132.5 0.0 copy-start.3
  132.5 0.0 copy-done.7
  132.5 2.6 %multiply_reduce_fusion.1 = (f32[]{:T(128)}, f32[512,512]{1,0:T(8,128)}) fusion(f32[512,512]{1,0:T(8,128)S(1)} %get-tuple-element.7, f32[1,1,1,512,512]{4,3,2,1,0:T(8,128)S(1)} %copy-done.7), kind=kOutput, calls=%fused_computation.16 | convolution fusion | flops 806617088 | bytes 3145732 | tf_op jit(solution)/shard_map/dot_general | solution.py:401
  135.8 1.1 fusion.8
  136.9 1.0 fusion.42
  137.9 2.0 fusion.2
  140.0 0.0 copy-done.3
  140.0 2.2 fusion.10
  142.2 0.0 copy-start.4
  142.2 2.0 fusion.43
  144.8 0.0 copy-done.4
  144.8 1.1 fusion.4
  145.9 1.0 fusion.44
  146.9 2.0 fusion.3
  148.9 0.0 copy-start.5
  149.0 2.3 %fusion.6 = f32[512,512]{1,0:T(8,128)S(1)} fusion(f32[512,512]{1,0:T(8,128)} %fusion.3, f32[512,512]{1,0:T(8,128)S(1)} %copy-done.4, f32[]{:T(128)S(6)} %mul.83, f32[]{:T(128)S(6)} %div.30), kind=kOutput, calls=%fused_computation.14 | convolution fusion | flops 806617088 | bytes 3145736 | tf_op jit(solution)/shard_map/dot_general | solution.py:401
  151.3 0.0 copy-done.5
  151.3 1.7 multiply_reduce_fusion
  153.1 74.6 %psum.7 = f32[]{:T(128)} all-reduce(f32[]{:T(128)} %get-tuple-element.12), channel_id=1, replica_groups=mesh['dp'=16,'mp'=4,'pre'=4] {'dp','mp','pre'}, use_global_device_ids=true, to_apply=%region_3.0 | all-reduce | flops 1 | bytes 8 | tf_op jit(solution)/shard_map/psum | solution.py:425
  228.3 1.1 divide_bitcast_fusion
  229.4 0.8 copy.10
Async XLA Ops:
  0.6 1.6 copy-start
  2.2 1.0 copy-start.1
  3.3 1.0 copy-start.2
  4.3 126.3 %copy-start.6 = (f32[1,1,1,512,512]{4,3,2,1,0:T(8,128)S(1)}, f32[1,1,1,512,512]{4,3,2,1,0:T(8,128)}, u32[]{:S(2)}) copy-start(f32[1,1,1,512,512]{4,3,2,1,0:T(8,128)} %param.8) | copy-start | bytes 3145732
  130.7 1.8 copy-start.7
  132.5 7.5 %copy-start.3 = (f32[512,512]{1,0:T(8,128)}, f32[512,512]{1,0:T(8,128)S(1)}, u32[]{:S(2)}) copy-start(f32[512,512]{1,0:T(8,128)S(1)} %get-tuple-element.9) | copy-start | bytes 3145732
  142.2 2.6 %copy-start.4 = (f32[512,512]{1,0:T(8,128)S(1)}, f32[512,512]{1,0:T(8,128)}, u32[]{:S(2)}) copy-start(f32[512,512]{1,0:T(8,128)} %get-tuple-element.11) | copy-start | bytes 3145732
  148.9 2.4 %copy-start.5 = (f32[512,512]{1,0:T(8,128)S(1)}, f32[512,512]{1,0:T(8,128)}, u32[]{:S(2)}) copy-start(f32[512,512]{1,0:T(8,128)} %fusion.43) | copy-start | bytes 3145732

commit v2 on v1

v2 whole, which is shorter than its diff:
```python
import jax
import jax.numpy as jnp
from jax import lax
from jax.experimental import pallas as pl
from jax.experimental.pallas import tpu as pltpu
from jax.sharding import PartitionSpec as P

D = 4096
FF = 16384
TOKENS = 4096
BLOCK = 512
NX, NY, NZ = 4, 4, 8

DECAY_RATE = 0.9
MESH = pl.DeviceIdType.MESH
DMA = pltpu.SemaphoreType.DMA
C0, C1, C2, C3 = 25 / 16, -(5 + 3125 / 256) / 16, 3125 / 4096, -1250 / 4096
C4, C5, C6 = 250 / 4096, -25 / 4096, 1 / 4096


def split(value):
    high = value.astype(jnp.bfloat16)
    return high, (value - high.astype(jnp.float32)).astype(jnp.bfloat16)


NN = (((1,), (0,)), ((), ()))
NT = (((1,), (1,)), ((), ()))
TN = (((0,), (0,)), ((), ()))


def dot(a, b, dims):
    return lax.dot_general(a, b, dims, preferred_element_type=jnp.float32)


def product(a, b, dims=NN):
    ah, al = a
    bh, bl = b
    return dot(ah, bh, dims) + (dot(ah, bl, dims) + dot(al, bh, dims))


def whole_kernel(
    act, cot, wblk, lstat, rstat,
    ig_out, left_out, right_out, update_out,
    ACT, OUTB, COT, CIG, WB, ACC, OB, G, GS, STAT, T2, T3, MS, CS, PS, RAW, RED,
    loc_sem, a1_s, a1_r, a1o_s, a1o_r, tz_s, tz_r, sw_s, sw_r,
    b1_s, b1_r, pa_s, pa_r, ring_s, ring_r, c1_s, c1_r, w_s, w_r, ws_s, ws_r, o_s, o_r,
    red_s, red_r, st_sem,
):
    dp = lax.axis_index("dp")
    y = lax.axis_index("mp")
    pre = lax.axis_index("pre")
    x = lax.div(dp, 4)
    zh = lax.rem(dp, 4)
    zl = lax.div(pre, 2)
    c = lax.rem(pre, 2)
    oc = 1 - c
    z = zh * 2 + zl
    grp = lax.div(z, 4)
    g = lax.rem(z, 4)
    side = lax.div(g, 2)
    inner = lax.rem(lax.div(g + 1, 2), 2)
    d = 1 - 2 * side
    so, sn, sf, se = 1 + side, 3 * side, 2 - side, 3 - 3 * side
    hpar = lax.rem(zh, 2)

    def dev(xx, yy, zz, cc):
        return {
            "dp": xx * 4 + lax.div(zz, 2),
            "mp": yy,
            "pre": lax.rem(zz, 2) * 2 + cc,
        }

    def xp(k):
        return lax.rem(x + k + 4, 4)

    def yp(k):
        return lax.rem(y + k + 4, 4)

    def zp(k):
        return lax.rem(z + k + 8, 8)

    def zp_d(sign):
        return lax.rem(z + sign * d + 8, 8)

    other = dev(x, y, z, oc)

    barrier = pltpu.get_barrier_semaphore()
    count = 0

    def greet(device):
        pl.semaphore_signal(barrier, inc=1, device_id=device, device_id_type=MESH)

    for k in range(4):
        for m in range(4):
            if k or m:
                greet({"dp": xp(k) * 4 + zh, "mp": y, "pre": lax.rem(pre + m, 4)})
                count += 1
    for k in range(1, 4):
        greet(dev(x, yp(k), z, c))
        count += 1
    pair = lax.rem(z + 1 - 2 * zl + 8, 8)
    for k in range(1, 7):
        greet(dev(x, y, lax.rem(pair + (1 - 2 * zl) * k + 16, 8), c))
        count += 1
    pl.semaphore_wait(barrier, count)

    sends = []

    def remote(src, dst, ssem, rsem, device, when=None):
        cp = pltpu.make_async_remote_copy(
            src_ref=src, dst_ref=dst, send_sem=ssem, recv_sem=rsem,
            device_id=device, device_id_type=MESH,
        )
        if when is None:
            cp.start()
        else:
            @pl.when(when)
            def _():
                cp.start()
        sends.append((when, cp))

    def arrived(dst, rsem):
        pltpu.make_async_copy(dst, dst, rsem).wait()

    is_inner = inner == 1
    is_outer = inner == 0

    def act_src(xx, gg):
        return act.at[
            pl.ds(pl.multiple_of(c * 128, 128), 128),
            pl.ds(pl.multiple_of(xx * 1024 + gg * 512, 512), 512),
        ]

    rel = (0, -1, 1, 2)
    xs = [xp(r) for r in rel]
    cot_piece = lambda half: cot.at[
        pl.ds(pl.multiple_of(y * 64, 64), 64),
        pl.ds(pl.multiple_of(half * 512, 512), 512),
    ]
    ypair = lax.div(y, 2)
    ylow = lax.rem(y, 2)
    cot_slot = lambda zz: COT.at[zz, ypair, x, ylow]
    pltpu.make_async_copy(cot_piece(hpar), cot_slot(zh), loc_sem.at[0]).start()
    remote(cot_piece(hpar), cot_slot(zh), b1_s.at[0], b1_r.at[0], dev(x, y, zp(4), c))
    remote(cot_piece(1 - hpar), cot_slot(zh), b1_s.at[1], b1_r.at[1], dev(x, y, zp(2), c))
    remote(cot_piece(1 - hpar), cot_slot(zh), b1_s.at[2], b1_r.at[2], dev(x, y, zp(-2), c))
    pltpu.make_async_copy(act_src(x, grp), ACT.at[so, c, x], loc_sem.at[1]).start()

    @pl.when(is_outer)
    def _():
        pltpu.make_async_copy(act_src(x, 1 - grp), OUTB.at[x], loc_sem.at[2]).start()

    for k, step in ((1, 1), (2, -1), (3, 2)):
        to = xp(step)
        remote(act_src(to, 1 - grp), OUTB.at[x], a1o_s.at[k], a1o_r.at[k],
               dev(to, y, z, c), when=is_outer)
        remote(act_src(to, grp), ACT.at[so, c, x], a1_s.at[k], a1_r.at[k], dev(to, y, z, c))
    cig_src = lambda q: cot.at[pl.ds(pl.multiple_of(q * 64, 64), 64), :]
    pltpu.make_async_copy(cig_src(pre), CIG.at[pre, x], loc_sem.at[3]).start()
    for k in range(1, 4):
        q = lax.rem(pre + k, 4)
        remote(cig_src(q), CIG.at[pre, x], c1_s.at[k], c1_r.at[k],
               {"dp": dp, "mp": y, "pre": q})
    pltpu.make_async_copy(wblk, WB.at[z, c], loc_sem.at[4]).start()
    remote(wblk, WB.at[z, c], ws_s.at[0], ws_r.at[0], other)

    def ring_start(base, unit, my, to_next, to_prev):
        for hf in range(2):
            remote(unit(my, hf), unit(my, hf), ring_s.at[base + hf], ring_r.at[base + hf], to_next)
            back = 1 - hf
            remote(unit(my, back), unit(my, back), ring_s.at[base + 2 + back],
                   ring_r.at[base + 2 + back], to_prev)

    def ring_forward(base, unit, prv, nxt, to_next, to_prev):
        arrived(unit(prv, 0), ring_r.at[base])
        remote(unit(prv, 0), unit(prv, 0), ring_s.at[base + 4], ring_r.at[base + 4], to_next)
        arrived(unit(nxt, 1), ring_r.at[base + 3])
        remote(unit(nxt, 1), unit(nxt, 1), ring_s.at[base + 5], ring_r.at[base + 5], to_prev)

    def ring_end(base, unit, prv, nxt, far):
        arrived(unit(prv, 1), ring_r.at[base + 1])
        arrived(unit(nxt, 0), ring_r.at[base + 2])
        arrived(unit(far, 0), ring_r.at[base + 4])
        arrived(unit(far, 1), ring_r.at[base + 5])

    xnext, xprev = dev(xp(1), y, z, c), dev(xp(-1), y, z, c)
    ynext, yprev = dev(x, yp(1), z, c), dev(x, yp(-1), z, c)
    u1a = lambda i: COT.at[pl.ds(0, 2), ypair, i, ylow]
    u2a = lambda i: COT.at[pl.ds(2, 2), lax.div(i, 2), x, lax.rem(i, 2)]
    u1b = lambda i, lo: COT.at[lo, lax.div(i, 2), :, lax.rem(i, 2)]
    u2b = lambda i, lo: COT.at[2 + lo, :, i]
    uc = lambda i, lo: CIG.at[pl.ds(2 * lo, 2), i]
    xargs = (xp(-1), xp(1), xnext, xprev)
    yargs = (yp(-1), yp(1), ynext, yprev)

    def cot_along_z():
        pltpu.make_async_copy(cot_piece(hpar), cot_slot(zh), loc_sem.at[0]).wait()
        arrived(cot_slot(lax.rem(zh + 3, 4)), b1_r.at[1])
        arrived(cot_slot(lax.rem(zh + 1, 4)), b1_r.at[2])
        arrived(cot_slot(lax.rem(zh + 2, 4)), b1_r.at[0])
        for k in (2, 1, 3):
            remote(u1a(x), u1a(x), pa_s.at[0, k], pa_r.at[0, k], dev(xp(k), y, z, c))
            remote(u2a(y), u2a(y), pa_s.at[1, k], pa_r.at[1, k], dev(x, yp(k), z, c))

    def cot_first():
        for k in (1, 3, 2):
            arrived(u1a(xp(-k)), pa_r.at[0, k])
            arrived(u2a(yp(-k)), pa_r.at[1, k])
        ring_start(0, u1b, y, ynext, yprev)
        ring_start(6, u2b, x, xnext, xprev)

    def cot_forward():
        ring_forward(0, u1b, *yargs)
        ring_forward(6, u2b, *xargs)

    def cot_end():
        ring_end(0, u1b, yp(-1), yp(1), yp(2))
        ring_end(6, u2b, xp(-1), xp(1), xp(2))

    def cig_first():
        pltpu.make_async_copy(cig_src(pre), CIG.at[pre, x], loc_sem.at[3]).wait()
        for k in range(1, 4):
            arrived(CIG.at[lax.rem(pre + 4 - k, 4), x], c1_r.at[k])
        ring_start(12, uc, x, xnext, xprev)

    def cig_forward():
        ring_forward(12, uc, *xargs)

    def cig_end():
        ring_end(12, uc, xp(-1), xp(1), xp(2))

    inward = dev(x, y, zp_d(1), c)
    outward = dev(x, y, zp_d(-1), c)
    kind_n = 2 * inner

    def swap(kind, k, slot):
        piece = ACT.at[slot, c, xs[k]]
        remote(piece, piece, sw_s.at[kind, k], sw_r.at[kind, k], other)

    def own(k):
        piece = ACT.at[so, c, xs[k]]
        if k == 0:
            pltpu.make_async_copy(act_src(x, grp), piece, loc_sem.at[1]).wait()

            @pl.when(is_outer)
            def _():
                pltpu.make_async_copy(act_src(x, 1 - grp), OUTB.at[x], loc_sem.at[2]).wait()
        else:
            @pl.when(is_outer)
            def _():
                arrived(OUTB.at[xs[k]], a1o_r.at[k])

        remote(OUTB.at[xs[k]], ACT.at[3 - sn, c, xs[k]],
               tz_s.at[0, k], tz_r.at[0, k], outward, when=is_outer)
        if k:
            arrived(piece, a1_r.at[k])
        remote(piece, piece, tz_s.at[1, k], tz_r.at[1, k], inward, when=is_inner)
        swap(3, k, so)

    def near(k):
        piece = ACT.at[sn, c, xs[k]]
        arrived(piece, tz_r.at[0, k])
        remote(piece, piece, tz_s.at[2, k], tz_r.at[kind_n, k], inward)
        swap(0, k, sn)

    def far(k):
        piece = ACT.at[sf, c, xs[k]]
        arrived(piece, tz_r.at[1, k])
        remote(piece, piece, tz_s.at[3, k], tz_r.at[1, k], outward, when=is_inner)
        swap(1, k, sf)

    def end(k):
        piece = ACT.at[se, c, xs[k]]
        arrived(piece, tz_r.at[2, k])
        remote(piece, piece, tz_s.at[4, k], tz_r.at[2, k], outward, when=is_inner)
        swap(2, k, se)

    znext, zprev = dev(x, y, zp(1), c), dev(x, y, zp(-1), c)
    wpart = lambda zz, hf: WB.at[zz, c, pl.ds(hf * 256, 256)]

    def w_send(way, t, hf):
        zz = zp(-(t - 1)) if way == 0 else zp(t - 1)
        remote(wblk.at[pl.ds(hf * 256, 256)] if t == 1 else wpart(zz, hf), wpart(zz, hf),
               w_s.at[way, t, hf], w_r.at[way, t, hf], znext if way == 0 else zprev)

    def w_index(way, t, hf):
        return 1 + (way * 5 + t) * 2 + hf

    def w_arrive(way, t, hf):
        zz = zp(-t) if way == 0 else zp(t)
        arrived(wpart(zz, hf), w_r.at[way, t, hf])
        if t < 3 or (t == 3 and hf == way):
            w_send(way, t + 1, hf)
        n = w_index(way, t, hf)
        remote(wpart(zz, hf), wpart(zz, hf), ws_s.at[n], ws_r.at[n], other)

    def w_first():
        for hf in range(2):
            for way in range(2):
                w_send(way, 1, hf)

    def w_step(t):
        for hf in range(2):
            for way in range(2):
                if t < 4 or hf == way:
                    w_arrive(way, t, hf)

    def ig_chip(zz):
        for cc in range(2):
            p = lax.rem(zz, 2) * 2 + cc
            h = lax.rem(lax.div(zz, 2), 2)
            a = CIG[p, :, :, pl.ds(pl.multiple_of(h * 512, 512), 512)].reshape(256, 512)
            ACC[lax.div(zz, 4)] += dot(a, WB[zz, cc], NT)

    def ig_own():
        pltpu.make_async_copy(wblk, WB.at[z, c], loc_sem.at[4]).wait()
        arrived(WB.at[z, oc], ws_r.at[0])
        ACC[...] = jnp.zeros_like(ACC)
        ig_chip(z)

    def ig_step(t):
        for way in range(2):
            zz = zp(-t) if way == 0 else zp(t)
            for hf in range(2):
                if t < 4 or hf == way:
                    arrived(WB.at[zz, oc, pl.ds(hf * 256, 256)], ws_r.at[w_index(way, t, hf)])
            if t < 4:
                ig_chip(zz)
        if t == 4:
            ig_chip(zp(4))

    def gradient():
        for kind, slot in ((3, so), (0, sn), (1, sf), (2, se)):
            for k in range(4):
                arrived(ACT.at[slot, oc, xs[k]], sw_r.at[kind, k])
        G[...] = jnp.zeros_like(G)

        @pl.loop(0, 8)
        def _(i):
            s = lax.div(i, 2)
            cc = lax.rem(i, 2)
            shard = lax.rem(2 * grp + 3 + s, 4)
            a = ACT[s, cc].reshape(BLOCK, BLOCK)
            b = COT[shard, cc].reshape(BLOCK, BLOCK)
            G[...] += dot(a, b, TN)

        grad = G[...] * (1.0 / TOKENS)
        high, low = split(grad)
        GS[0] = high
        GS[1] = low

    pair_of = lambda ref: (ref[0], ref[1])

    def put(ref, value):
        high, low = split(value)
        ref[0] = high
        ref[1] = low

    def statistic(i, dims, old, new):
        pltpu.make_async_copy(old, STAT.at[i], st_sem.at[i]).wait()
        g = pair_of(GS)
        STAT[i] = DECAY_RATE * STAT[i] + (1.0 - DECAY_RATE) * product(g, g, dims)
        cp = pltpu.make_async_copy(STAT.at[i], new, st_sem.at[2 + i])
        cp.start()
        local_out.append(cp)

    scale = [None, None]

    def root_1(i):
        a = STAT[i]
        z_of = 2.5 * lax.rsqrt(jnp.sum(a * a, axis=(0, 1), keepdims=True))
        scale[i] = z_of
        put(MS, z_of * a)
        T2[...] = product(pair_of(MS), pair_of(MS))
        put(CS, T2[...])

    def root_2(i):
        T3[...] = product(pair_of(MS), pair_of(CS))

    def root_3(i):
        m = scale[i] * STAT[i]
        put(CS, C4 * m + C5 * T2[...] + C6 * T3[...])
        put(MS, T3[...])
        eye = (
            lax.broadcasted_iota(jnp.int32, (BLOCK, BLOCK), 0)
            == lax.broadcasted_iota(jnp.int32, (BLOCK, BLOCK), 1)
        )
        low_part = C1 * m + C2 * T2[...] + C3 * T3[...] + jnp.where(eye, C0, 0.0)
        whole = low_part + product(pair_of(MS), pair_of(CS))
        put(PS.at[i], jnp.sqrt(jnp.sqrt(scale[i])) * whole)

    def raw_1():
        put(CS, product(pair_of(PS.at[0]), pair_of(GS)))

    def raw_2():
        raw = product(pair_of(CS), pair_of(PS.at[1]))
        RAW[...] = raw
        RED[0] = jnp.broadcast_to(jnp.sum(raw * raw, axis=(0, 1), keepdims=True), (8, 128))

    def red_targets(stage):
        if stage == 0:
            return [(1, other)]
        if stage == 1:
            return [(1 + k, dev(x, y, zp(k), c)) for k in range(1, 8)]
        if stage == 2:
            return [(8 + k, dev(xp(k), y, z, c)) for k in range(1, 4)]
        return [(11 + k, dev(x, yp(k), z, c)) for k in range(1, 4)]

    def red_send(stage):
        for slot, device in red_targets(stage):
            remote(RED.at[15 + stage], RED.at[slot], red_s.at[slot], red_r.at[slot], device)

    def red_start(stage):
        RED[15 + stage] = RED[0]
        red_send(stage)

    def red_finish(stage):
        total = RED[0]
        for slot, _ in red_targets(stage):
            arrived(RED.at[slot], red_r.at[slot])
            total = total + RED[slot]
        RED[0] = total

    def update():
        mean_square = RED[0, 0:1, 0:1] * (1.0 / (FF * D))
        RAW[...] = RAW[...] * lax.rsqrt(mean_square + 1e-06)
        cp = pltpu.make_async_copy(RAW, update_out, st_sem.at[4])
        cp.start()
        local_out.append(cp)

    local_out = []
    pltpu.make_async_copy(lstat, STAT.at[0], st_sem.at[0]).start()
    pltpu.make_async_copy(rstat, STAT.at[1], st_sem.at[1]).start()

    own(0)
    w_first()
    cot_along_z()
    own(1)
    own(2)
    near(0)
    cot_first()
    far(0)
    near(1)
    own(3)
    near(2)
    far(1)
    end(0)
    cot_forward()
    w_step(1)
    near(3)
    far(2)
    end(1)
    cig_first()
    far(3)
    end(2)
    end(3)
    cot_end()
    w_step(2)
    cig_forward()
    gradient()
    statistic(0, NT, lstat, left_out)
    statistic(1, TN, rstat, right_out)
    root_1(0)
    root_2(0)
    w_step(3)
    root_3(0)
    root_1(1)
    root_2(1)
    root_3(1)
    raw_1()
    raw_2()
    red_start(0)
    cig_end()
    red_finish(0)
    red_start(1)
    ig_own()
    ig_step(1)
    red_finish(1)
    red_start(2)
    ig_step(2)
    red_finish(2)
    red_start(3)
    ig_step(3)
    red_finish(3)
    update()
    w_step(4)
    ig_step(4)

    for j in range(2):
        OB[:, :, pl.ds(j * 512, 512)] = ACC[j].reshape(4, 64, 512).astype(jnp.bfloat16)
    sub = zl * 2 + c
    z_to = zh * 2 + lax.div(x, 2)
    c_to = lax.rem(x, 2)
    rows = ig_out.at[pl.ds(pl.multiple_of(sub * 64, 64), 64), :]
    mine = pre == x
    for k in range(4):
        xt = xs[k]
        dst = dev(xt, y, z_to, c_to)
        if k == 0:
            remote(OB.at[xt], rows, o_s.at[k], o_r.at[sub], dst, when=jnp.logical_not(mine))

            @pl.when(mine)
            def _():
                cp = pltpu.make_async_copy(OB.at[x], rows, loc_sem.at[5])
                cp.start()
                cp.wait()
        else:
            remote(OB.at[xt], rows, o_s.at[k], o_r.at[sub], dst)
    for q in range(4):
        piece = ig_out.at[pl.ds(q * 64, 64), :]

        @pl.when(jnp.logical_not(jnp.logical_and(mine, sub == q)))
        def _():
            arrived(piece, o_r.at[q])

    for cp in local_out:
        cp.wait()
    for when, cp in sends:
        if when is None:
            cp.wait_send()
        else:
            pl.when(when)(cp.wait_send)


def whole_call(act, cot, wblk, lstat, rstat):
    any_spec = pl.BlockSpec(memory_space=pl.ANY)
    bf, f32 = jnp.bfloat16, jnp.float32
    square = jax.ShapeDtypeStruct((BLOCK, BLOCK), f32)
    return pl.pallas_call(
        whole_kernel,
        out_shape=(jax.ShapeDtypeStruct((256, 1024), bf), square, square, square),
        in_specs=[any_spec] * 5,
        out_specs=(any_spec,) * 4,
        scratch_shapes=[
            pltpu.VMEM((4, 2, 4, 128, 512), bf),
            pltpu.VMEM((4, 128, 512), bf),
            pltpu.VMEM((4, 2, 4, 2, 64, 512), bf),
            pltpu.VMEM((4, 4, 64, 1024), bf),
            pltpu.VMEM((8, 2, 512, 512), bf),
            pltpu.VMEM((2, 256, 512), f32),
            pltpu.VMEM((4, 64, 1024), bf),
            pltpu.VMEM((BLOCK, BLOCK), f32),
            pltpu.VMEM((2, BLOCK, BLOCK), bf),
            pltpu.VMEM((2, BLOCK, BLOCK), f32),
            pltpu.VMEM((BLOCK, BLOCK), f32),
            pltpu.VMEM((BLOCK, BLOCK), f32),
            pltpu.VMEM((2, BLOCK, BLOCK), bf),
            pltpu.VMEM((2, BLOCK, BLOCK), bf),
            pltpu.VMEM((2, 2, BLOCK, BLOCK), bf),
            pltpu.VMEM((BLOCK, BLOCK), f32),
            pltpu.VMEM((19, 8, 128), f32),
            DMA((6,)), DMA((4,)), DMA((4,)), DMA((4,)), DMA((4,)),
            DMA((5, 4)), DMA((3, 4)), DMA((4, 4)), DMA((4, 4)),
            DMA((3,)), DMA((3,)), DMA((2, 4)), DMA((2, 4)), DMA((18,)), DMA((18,)),
            DMA((4,)), DMA((4,)), DMA((2, 5, 2)), DMA((2, 5, 2)), DMA((21,)), DMA((21,)),
            DMA((4,)), DMA((4,)), DMA((15,)), DMA((15,)), DMA((5,)),
        ],
        compiler_params=pltpu.CompilerParams(
            collective_id=0, has_side_effects=True, vmem_limit_bytes=60 * 1024 * 1024
        ),
        name="gather_products",
    )(act, cot, wblk, lstat, rstat)


def on_device(activations, cotangent, weight_blocks, left_stat, right_stat):
    square = (BLOCK, BLOCK)
    input_grad, left_next, right_next, update = whole_call(
        activations,
        cotangent,
        weight_blocks.reshape(square),
        left_stat.reshape(square),
        right_stat.reshape(square),
    )
    shape_out = left_stat.shape
    return (
        input_grad,
        left_next.reshape(shape_out),
        right_next.reshape(shape_out),
        update.reshape(shape_out),
    )


def solution(mesh):
    block = P("dp", "mp", "pre", None, None)
    return jax.shard_map(
        on_device,
        mesh=mesh,
        in_specs=(P("dp", "mp"), P("dp", "pre"), block, block, block),
        out_specs=(P("dp", ("mp", "pre")), block, block, block),
        check_vma=False,
    )
```

time: 232 us -> 138 us (0.59)
  blocking collectives: 74.6 us -> 0 us
  matrix products: 20.9 us -> 0 us
  Pallas kernels: 126 us -> 130 us
    psum x1 -> x0, blocking collectives: 74.6 us -> none  [on_device(): square_sum = lax.psum(jnp.sum(raw_update * raw_update), ('dp', 'mp', 'pre'))]
    dot_general x12 -> x0, matrix products: 20.9 us -> none  [product(): jnp.dot(former, latter, precision=HIGH, preferred_element_type=jnp.float32)]
    pallas_call x1, Pallas kernels: 126 us -> 130 us  [whole_call(): pl.pallas_call(whole_kernel, out_shape=(jax.ShapeDtypeStruct((256, 1024),...]
    unnamed x17 -> x8, local copies, waits for them, and re-layouts: 4.48 us -> 6.25 us
where the time goes in v2:
time: 138 us; the launch traced here: 137 us
  Pallas kernels  130 us (94%)
  local copies, waits for them, and re-layouts  6.25 us (5%)
    pallas_call x1, Pallas kernels, whole_call(): pl.pallas_call(whole_kernel, out_shape=(jax.ShapeDtypeStruct((256, 1024),...  130 us
    unnamed x8, local copies, waits for them, and re-layouts  6.25 us

profile of v2, /device:TPU:32, one launch (start us, length us, event | category | flops | bytes accessed | tf_op | source)
XLA Modules:
  0.0 137.4 jit_solution(6636288866651594853)
XLA Ops:
  0.6 130.5 %gather_products.1 = (bf16[256,1024]{1,0:T(8,128)(2,1)}, f32[512,512]{1,0:T(8,128)}, f32[512,512]{1,0:T(8,128)}, f32[512,512]{1,0:T(8,128)}) custom-call(bf16[256,4096]{1,0:T(8,128)(2,1)} %act.1, bf16[256,1024]{1,0:T(8,128)(2,1)} %cot.1, bf16[512,512]{1,0:T(8,128)(2,1)} %bitcast.11, f32[512,512]{1,0:T(8,128)} %bitcast.6, f32[512,512]{1,0:T(8,128)} %bitcast.7), custom_call_target="tpu_custom_call" | custom-call | tf_op jit(solution)/shard_map/gather_products/pallas_call | solution.py:529
  131.1 0.0 copy-start.1
  131.1 2.0 %copy.13 = bf16[256,1024]{1,0:T(8,128)(2,1)} copy(bf16[256,1024]{1,0:T(8,128)(2,1)} %get-tuple-element.16) | data formatting | bytes 1048576
  133.1 0.0 copy-start
  133.1 2.4 %copy.14 = f32[1,1,1,512,512]{4,3,2,1,0:T(8,128)} copy(f32[1,1,1,512,512]{4,3,2,1,0:T(8,128)} %bitcast.10) | data formatting | bytes 2097152
  135.4 0.0 copy-done.1
  135.4 1.0 copy.15
  136.4 0.0 copy-done
  136.4 1.0 copy.16
Async XLA Ops:
  131.1 4.3 %copy-start.1 = (f32[512,512]{1,0:T(8,128)S(1)}, f32[512,512]{1,0:T(8,128)}, u32[]{:S(2)}) copy-start(f32[512,512]{1,0:T(8,128)} %get-tuple-element.10) | copy-start | bytes 3145732
  133.1 3.3 %copy-start = (f32[512,512]{1,0:T(8,128)S(1)}, f32[512,512]{1,0:T(8,128)}, u32[]{:S(2)}) copy-start(f32[512,512]{1,0:T(8,128)} %get-tuple-element.11) | copy-start | bytes 3145732

commit v3 on v2

--- a/solution.py
+++ b/solution.py
@@ -1,3 +1,5 @@
+import math
+
 import jax
 import jax.numpy as jnp
 from jax import lax
@@ -105,19 +107,19 @@
     pl.semaphore_wait(barrier, count)
 
     sends = []
+    branch = [None]
 
     def remote(src, dst, ssem, rsem, device, when=None):
         cp = pltpu.make_async_remote_copy(
-            src_ref=src, dst_ref=dst, send_sem=ssem, recv_sem=rsem,
+            src_ref=src, dst_ref=dst, send_sem=ssem[0].at[ssem[1]], recv_sem=rsem,
             device_id=device, device_id_type=MESH,
         )
         if when is None:
             cp.start()
         else:
-            @pl.when(when)
-            def _():
-                cp.start()
-        sends.append((when, cp))
+            pl.when(when)(cp.start)
+        size = math.prod(dst.shape)
+        sends.append((branch[0] if when is None else when, size, ssem))
 
     def arrived(dst, rsem):
         pltpu.make_async_copy(dst, dst, rsem).wait()
@@ -141,41 +143,46 @@
     ylow = lax.rem(y, 2)
     cot_slot = lambda zz: COT.at[zz, ypair, x, ylow]
     pltpu.make_async_copy(cot_piece(hpar), cot_slot(zh), loc_sem.at[0]).start()
-    remote(cot_piece(hpar), cot_slot(zh), b1_s.at[0], b1_r.at[0], dev(x, y, zp(4), c))
-    remote(cot_piece(1 - hpar), cot_slot(zh), b1_s.at[1], b1_r.at[1], dev(x, y, zp(2), c))
-    remote(cot_piece(1 - hpar), cot_slot(zh), b1_s.at[2], b1_r.at[2], dev(x, y, zp(-2), c))
-    pltpu.make_async_copy(act_src(x, grp), ACT.at[so, c, x], loc_sem.at[1]).start()
-
-    @pl.when(is_outer)
-    def _():
-        pltpu.make_async_copy(act_src(x, 1 - grp), OUTB.at[x], loc_sem.at[2]).start()
-
-    for k, step in ((1, 1), (2, -1), (3, 2)):
-        to = xp(step)
-        remote(act_src(to, 1 - grp), OUTB.at[x], a1o_s.at[k], a1o_r.at[k],
-               dev(to, y, z, c), when=is_outer)
-        remote(act_src(to, grp), ACT.at[so, c, x], a1_s.at[k], a1_r.at[k], dev(to, y, z, c))
-    cig_src = lambda q: cot.at[pl.ds(pl.multiple_of(q * 64, 64), 64), :]
-    pltpu.make_async_copy(cig_src(pre), CIG.at[pre, x], loc_sem.at[3]).start()
-    for k in range(1, 4):
-        q = lax.rem(pre + k, 4)
-        remote(cig_src(q), CIG.at[pre, x], c1_s.at[k], c1_r.at[k],
-               {"dp": dp, "mp": y, "pre": q})
-    pltpu.make_async_copy(wblk, WB.at[z, c], loc_sem.at[4]).start()
-    remote(wblk, WB.at[z, c], ws_s.at[0], ws_r.at[0], other)
+    remote(cot_piece(hpar), cot_slot(zh), (b1_s, (0,)), b1_r.at[0], dev(x, y, zp(4), c))
+    remote(cot_piece(1 - hpar), cot_slot(zh), (b1_s, (1,)), b1_r.at[1], dev(x, y, zp(2), c))
+    remote(cot_piece(1 - hpar), cot_slot(zh), (b1_s, (2,)), b1_r.at[2], dev(x, y, zp(-2), c))
+    cig_src = lambda q: cot.at[pl.ds(pl.multiple_of(q * 64 + y * 16, 16), 16), :]
+
+    def cig_sends():
+        pltpu.make_async_copy(cig_src(pre), CIG.at[pre, x, y], loc_sem.at[3]).start()
+        for k in range(1, 4):
+            q = lax.rem(pre + k, 4)
+            remote(cig_src(q), CIG.at[pre, x, y], (c1_s, (k,)), c1_r.at[k],
+                   {"dp": dp, "mp": y, "pre": q})
+
+    def act_sends():
+        pltpu.make_async_copy(act_src(x, grp), ACT.at[so, c, x], loc_sem.at[1]).start()
+
+        @pl.when(is_outer)
+        def _():
+            pltpu.make_async_copy(act_src(x, 1 - grp), OUTB.at[x], loc_sem.at[2]).start()
+
+        steps = ((1, 1), (2, -1), (3, 2))
+        for k, step in steps:
+            to = xp(step)
+            remote(act_src(to, 1 - grp), OUTB.at[x], (a1o_s, (k,)), a1o_r.at[k],
+                   dev(to, y, z, c), when=is_outer)
+        for k, step in steps:
+            to = xp(step)
+            remote(act_src(to, grp), ACT.at[so, c, x], (a1_s, (k,)), a1_r.at[k], dev(to, y, z, c))
 
     def ring_start(base, unit, my, to_next, to_prev):
         for hf in range(2):
-            remote(unit(my, hf), unit(my, hf), ring_s.at[base + hf], ring_r.at[base + hf], to_next)
+            remote(unit(my, hf), unit(my, hf), (ring_s, (base + hf,)), ring_r.at[base + hf], to_next)
             back = 1 - hf
-            remote(unit(my, back), unit(my, back), ring_s.at[base + 2 + back],
+            remote(unit(my, back), unit(my, back), (ring_s, (base + 2 + back,)),
                    ring_r.at[base + 2 + back], to_prev)
 
     def ring_forward(base, unit, prv, nxt, to_next, to_prev):
         arrived(unit(prv, 0), ring_r.at[base])
-        remote(unit(prv, 0), unit(prv, 0), ring_s.at[base + 4], ring_r.at[base + 4], to_next)
+        remote(unit(prv, 0), unit(prv, 0), (ring_s, (base + 4,)), ring_r.at[base + 4], to_next)
         arrived(unit(nxt, 1), ring_r.at[base + 3])
-        remote(unit(nxt, 1), unit(nxt, 1), ring_s.at[base + 5], ring_r.at[base + 5], to_prev)
+        remote(unit(nxt, 1), unit(nxt, 1), (ring_s, (base + 5,)), ring_r.at[base + 5], to_prev)
 
     def ring_end(base, unit, prv, nxt, far):
         arrived(unit(prv, 1), ring_r.at[base + 1])
@@ -185,94 +192,118 @@
 
     xnext, xprev = dev(xp(1), y, z, c), dev(xp(-1), y, z, c)
     ynext, yprev = dev(x, yp(1), z, c), dev(x, yp(-1), z, c)
-    u1a = lambda i: COT.at[pl.ds(0, 2), ypair, i, ylow]
-    u2a = lambda i: COT.at[pl.ds(2, 2), lax.div(i, 2), x, lax.rem(i, 2)]
-    u1b = lambda i, lo: COT.at[lo, lax.div(i, 2), :, lax.rem(i, 2)]
-    u2b = lambda i, lo: COT.at[2 + lo, :, i]
-    uc = lambda i, lo: CIG.at[pl.ds(2 * lo, 2), i]
+    shards = [lax.rem(zh + r, 4) for r in range(4)]
+
+    def cot_unit(r, i, lo):
+        if r == 2:
+            return COT.at[shards[r], lo, i]
+        return COT.at[shards[r], lax.div(i, 2), pl.ds(2 * lo, 2), lax.rem(i, 2)]
+
+    uc = lambda i, lo: CIG.at[pl.ds(2 * lo, 2), :, i]
     xargs = (xp(-1), xp(1), xnext, xprev)
     yargs = (yp(-1), yp(1), ynext, yprev)
 
-    def cot_along_z():
-        pltpu.make_async_copy(cot_piece(hpar), cot_slot(zh), loc_sem.at[0]).wait()
-        arrived(cot_slot(lax.rem(zh + 3, 4)), b1_r.at[1])
-        arrived(cot_slot(lax.rem(zh + 1, 4)), b1_r.at[2])
-        arrived(cot_slot(lax.rem(zh + 2, 4)), b1_r.at[0])
+    def cot_a(r):
+        piece = cot_slot(shards[r])
+        if r:
+            arrived(piece, b1_r.at[{1: 2, 3: 1, 2: 0}[r]])
         for k in (2, 1, 3):
-            remote(u1a(x), u1a(x), pa_s.at[0, k], pa_r.at[0, k], dev(xp(k), y, z, c))
-            remote(u2a(y), u2a(y), pa_s.at[1, k], pa_r.at[1, k], dev(x, yp(k), z, c))
-
-    def cot_first():
+            to = dev(x, yp(k), z, c) if r == 2 else dev(xp(k), y, z, c)
+            remote(piece if r else cot_piece(hpar), piece, (pa_s, (r, k,)), pa_r.at[r, k], to)
+
+    def cot_b(r):
         for k in (1, 3, 2):
-            arrived(u1a(xp(-k)), pa_r.at[0, k])
-            arrived(u2a(yp(-k)), pa_r.at[1, k])
-        ring_start(0, u1b, y, ynext, yprev)
-        ring_start(6, u2b, x, xnext, xprev)
-
-    def cot_forward():
-        ring_forward(0, u1b, *yargs)
-        ring_forward(6, u2b, *xargs)
-
-    def cot_end():
-        ring_end(0, u1b, yp(-1), yp(1), yp(2))
-        ring_end(6, u2b, xp(-1), xp(1), xp(2))
-
-    def cig_first():
-        pltpu.make_async_copy(cig_src(pre), CIG.at[pre, x], loc_sem.at[3]).wait()
+            if r == 2:
+                arrived(COT.at[shards[r], lax.div(yp(-k), 2), x, lax.rem(yp(-k), 2)], pa_r.at[r, k])
+            else:
+                arrived(COT.at[shards[r], ypair, xp(-k), ylow], pa_r.at[r, k])
+        if r == 0:
+            pltpu.make_async_copy(cot_piece(hpar), cot_slot(zh), loc_sem.at[0]).wait()
+        unit = lambda i, lo: cot_unit(r, i, lo)
+        if r == 2:
+            ring_start(6 * r, unit, x, xnext, xprev)
+        else:
+            ring_start(6 * r, unit, y, ynext, yprev)
+
+    def cot_f(r):
+        unit = lambda i, lo: cot_unit(r, i, lo)
+        ring_forward(6 * r, unit, *(xargs if r == 2 else yargs))
+
+    def cot_e(r):
+        unit = lambda i, lo: cot_unit(r, i, lo)
+        m = xp if r == 2 else yp
+        ring_end(6 * r, unit, m(-1), m(1), m(2))
+
+    def cig_a():
+        pltpu.make_async_copy(cig_src(pre), CIG.at[pre, x, y], loc_sem.at[3]).wait()
         for k in range(1, 4):
-            arrived(CIG.at[lax.rem(pre + 4 - k, 4), x], c1_r.at[k])
-        ring_start(12, uc, x, xnext, xprev)
-
-    def cig_forward():
-        ring_forward(12, uc, *xargs)
-
-    def cig_end():
-        ring_end(12, uc, xp(-1), xp(1), xp(2))
+            arrived(CIG.at[lax.rem(pre + 4 - k, 4), x, y], c1_r.at[k])
+        for k in (2, 1, 3):
+            piece = CIG.at[:, x, y]
+            remote(piece, piece, (pa_s, (4, k)), pa_r.at[4, k], dev(xp(k), y, z, c))
+
+    def cig_b():
+        for k in (1, 3, 2):
+            arrived(CIG.at[:, xp(-k), y], pa_r.at[4, k])
+        ring_start(24, uc, y, ynext, yprev)
+
+    def cig_f():
+        ring_forward(24, uc, *yargs)
+
+    def cig_e():
+        ring_end(24, uc, yp(-1), yp(1), yp(2))
 
     inward = dev(x, y, zp_d(1), c)
     outward = dev(x, y, zp_d(-1), c)
-    kind_n = 2 * inner
 
     def swap(kind, k, slot):
         piece = ACT.at[slot, c, xs[k]]
-        remote(piece, piece, sw_s.at[kind, k], sw_r.at[kind, k], other)
+        remote(piece, piece, (sw_s, (kind, k,)), sw_r.at[kind, k], other)
 
     def own(k):
         piece = ACT.at[so, c, xs[k]]
+        if branch[0] is is_outer:
+            if k == 0:
+                pltpu.make_async_copy(act_src(x, 1 - grp), OUTB.at[x], loc_sem.at[2]).wait()
+            else:
+                arrived(OUTB.at[xs[k]], a1o_r.at[k])
+            remote(OUTB.at[xs[k]], ACT.at[3 - sn, c, xs[k]],
+                   (tz_s, (0, k,)), tz_r.at[0, k], outward)
+        else:
+            own_here(k, piece)
+            remote(piece, piece, (tz_s, (1, k,)), tz_r.at[1, k], inward)
+
+    def own_here(k, piece):
         if k == 0:
             pltpu.make_async_copy(act_src(x, grp), piece, loc_sem.at[1]).wait()
-
-            @pl.when(is_outer)
-            def _():
-                pltpu.make_async_copy(act_src(x, 1 - grp), OUTB.at[x], loc_sem.at[2]).wait()
         else:
-            @pl.when(is_outer)
-            def _():
-                arrived(OUTB.at[xs[k]], a1o_r.at[k])
-
-        remote(OUTB.at[xs[k]], ACT.at[3 - sn, c, xs[k]],
-               tz_s.at[0, k], tz_r.at[0, k], outward, when=is_outer)
-        if k:
             arrived(piece, a1_r.at[k])
-        remote(piece, piece, tz_s.at[1, k], tz_r.at[1, k], inward, when=is_inner)
+
+    def own_swap(k):
+        piece = ACT.at[so, c, xs[k]]
+        if branch[0] is is_outer:
+            own_here(k, piece)
         swap(3, k, so)
 
     def near(k):
         piece = ACT.at[sn, c, xs[k]]
         arrived(piece, tz_r.at[0, k])
-        remote(piece, piece, tz_s.at[2, k], tz_r.at[kind_n, k], inward)
+        remote(piece, piece, (tz_s, (2, k,)),
+               tz_r.at[0 if branch[0] is is_outer else 2, k], inward)
         swap(0, k, sn)
 
     def far(k):
         piece = ACT.at[sf, c, xs[k]]
         arrived(piece, tz_r.at[1, k])
-        remote(piece, piece, tz_s.at[3, k], tz_r.at[1, k], outward, when=is_inner)
+        if branch[0] is is_inner:
+            remote(piece, piece, (tz_s, (3, k,)), tz_r.at[1, k], outward)
         swap(1, k, sf)
 
     def end(k):
         piece = ACT.at[se, c, xs[k]]
         arrived(piece, tz_r.at[2, k])
-        remote(piece, piece, tz_s.at[4, k], tz_r.at[2, k], outward, when=is_inner)
+        if branch[0] is is_inner:
+            remote(piece, piece, (tz_s, (4, k,)), tz_r.at[2, k], outward)
         swap(2, k, se)
 
     znext, zprev = dev(x, y, zp(1), c), dev(x, y, zp(-1), c)
@@ -281,7 +312,7 @@
     def w_send(way, t, hf):
         zz = zp(-(t - 1)) if way == 0 else zp(t - 1)
         remote(wblk.at[pl.ds(hf * 256, 256)] if t == 1 else wpart(zz, hf), wpart(zz, hf),
-               w_s.at[way, t, hf], w_r.at[way, t, hf], znext if way == 0 else zprev)
+               (w_s, (way, t, hf,)), w_r.at[way, t, hf], znext if way == 0 else zprev)
 
     def w_index(way, t, hf):
         return 1 + (way * 5 + t) * 2 + hf
@@ -292,24 +323,25 @@
         if t < 3 or (t == 3 and hf == way):
             w_send(way, t + 1, hf)
         n = w_index(way, t, hf)
-        remote(wpart(zz, hf), wpart(zz, hf), ws_s.at[n], ws_r.at[n], other)
+        remote(wpart(zz, hf), wpart(zz, hf), (ws_s, (n,)), ws_r.at[n], other)
 
     def w_first():
+        pltpu.make_async_copy(wblk, WB.at[z, c], loc_sem.at[4]).start()
+        remote(wblk, WB.at[z, c], (ws_s, (0,)), ws_r.at[0], other)
         for hf in range(2):
             for way in range(2):
                 w_send(way, 1, hf)
 
-    def w_step(t):
-        for hf in range(2):
-            for way in range(2):
-                if t < 4 or hf == way:
-                    w_arrive(way, t, hf)
+    def w_half(t, hf):
+        for way in range(2):
+            if t < 4 or hf == way:
+                w_arrive(way, t, hf)
 
     def ig_chip(zz):
         for cc in range(2):
             p = lax.rem(zz, 2) * 2 + cc
             h = lax.rem(lax.div(zz, 2), 2)
-            a = CIG[p, :, :, pl.ds(pl.multiple_of(h * 512, 512), 512)].reshape(256, 512)
+            a = CIG[p, :, :, :, pl.ds(pl.multiple_of(h * 512, 512), 512)].reshape(256, 512)
             ACC[lax.div(zz, 4)] += dot(a, WB[zz, cc], NT)
 
     def ig_own():
@@ -318,14 +350,17 @@
         ACC[...] = jnp.zeros_like(ACC)
         ig_chip(z)
 
+    def ig_wait(way, t):
+        zz = zp(-t) if way == 0 else zp(t)
+        for hf in range(2):
+            if t < 4 or hf == way:
+                arrived(WB.at[zz, oc, pl.ds(hf * 256, 256)], ws_r.at[w_index(way, t, hf)])
+
     def ig_step(t):
         for way in range(2):
-            zz = zp(-t) if way == 0 else zp(t)
-            for hf in range(2):
-                if t < 4 or hf == way:
-                    arrived(WB.at[zz, oc, pl.ds(hf * 256, 256)], ws_r.at[w_index(way, t, hf)])
+            ig_wait(way, t)
             if t < 4:
-                ig_chip(zz)
+                ig_chip(zp(-t) if way == 0 else zp(t))
         if t == 4:
             ig_chip(zp(4))
 
@@ -408,7 +443,7 @@
 
     def red_send(stage):
         for slot, device in red_targets(stage):
-            remote(RED.at[15 + stage], RED.at[slot], red_s.at[slot], red_r.at[slot], device)
+            remote(RED.at[15 + stage], RED.at[slot], (red_s, (slot,)), red_r.at[slot], device)
 
     def red_start(stage):
         RED[15 + stage] = RED[0]
@@ -432,58 +467,123 @@
     pltpu.make_async_copy(lstat, STAT.at[0], st_sem.at[0]).start()
     pltpu.make_async_copy(rstat, STAT.at[1], st_sem.at[1]).start()
 
-    own(0)
+    cot_a(0)
+    act_sends()
+    cig_sends()
+
+    @pl.when(is_inner)
+    def _():
+        branch[0] = is_inner
+        own(0)
+        cot_b(0)
+        own(1)
+        own(2)
+        far(0)
+        cot_a(1)
+        cot_a(3)
+        own(3)
+        far(1)
+        near(0)
+        far(2)
+        cot_a(2)
+        cot_b(1)
+        near(1)
+        far(3)
+        cot_f(0)
+        cot_b(3)
+        near(2)
+        end(0)
+        cot_b(2)
+        near(3)
+        end(1)
+        cot_f(1)
+        end(2)
+        end(3)
+        cot_f(3)
+        cot_f(2)
+        cig_a()
+        own_swap(0)
+        own_swap(1)
+        own_swap(2)
+        own_swap(3)
+
+    @pl.when(is_outer)
+    def _():
+        branch[0] = is_outer
+        own(0)
+        cot_b(0)
+        own(1)
+        own(2)
+        cot_a(1)
+        cot_a(3)
+        own(3)
+        near(0)
+        near(1)
+        far(0)
+        cot_a(2)
+        cot_b(1)
+        near(2)
+        far(1)
+        cot_f(0)
+        near(3)
+        cot_b(3)
+        far(2)
+        end(0)
+        cot_b(2)
+        far(3)
+        end(1)
+        cot_f(1)
+        end(2)
+        end(3)
+        cot_f(3)
+        cot_f(2)
+        cig_a()
+        own_swap(0)
+        own_swap(1)
+        own_swap(2)
+        own_swap(3)
+
+    branch[0] = None
     w_first()
-    cot_along_z()
-    own(1)
-    own(2)
-    near(0)
-    cot_first()
-    far(0)
-    near(1)
-    own(3)
-    near(2)
-    far(1)
-    end(0)
-    cot_forward()
-    w_step(1)
-    near(3)
-    far(2)
-    end(1)
-    cig_first()
-    far(3)
-    end(2)
-    end(3)
-    cot_end()
-    w_step(2)
-    cig_forward()
+    cot_e(0)
+    cot_e(1)
+    cot_e(3)
+    cot_e(2)
+    cig_b()
     gradient()
     statistic(0, NT, lstat, left_out)
     statistic(1, TN, rstat, right_out)
+    w_half(1, 0)
     root_1(0)
     root_2(0)
-    w_step(3)
     root_3(0)
+    w_half(1, 1)
+    cig_f()
     root_1(1)
     root_2(1)
     root_3(1)
     raw_1()
+    w_half(2, 0)
     raw_2()
     red_start(0)
-    cig_end()
     red_finish(0)
     red_start(1)
+    cig_e()
     ig_own()
-    ig_step(1)
+    w_half(2, 1)
     red_finish(1)
     red_start(2)
-    ig_step(2)
+    ig_step(1)
+    w_half(3, 0)
     red_finish(2)
     red_start(3)
-    ig_step(3)
+    ig_step(2)
+    w_half(3, 1)
     red_finish(3)
     update()
-    w_step(4)
+    ig_step(3)
+    w_half(4, 0)
+    w_half(4, 1)
     ig_step(4)
 
     for j in range(2):
@@ -493,11 +593,12 @@
     c_to = lax.rem(x, 2)
     rows = ig_out.at[pl.ds(pl.multiple_of(sub * 64, 64), 64), :]
     mine = pre == x
+    not_mine = jnp.logical_not(mine)
     for k in range(4):
         xt = xs[k]
         dst = dev(xt, y, z_to, c_to)
         if k == 0:
-            remote(OB.at[xt], rows, o_s.at[k], o_r.at[sub], dst, when=jnp.logical_not(mine))
+            remote(OB.at[xt], rows, (o_s, (k,)), o_r.at[sub], dst, when=not_mine)
 
             @pl.when(mine)
             def _():
@@ -505,7 +606,7 @@
                 cp.start()
                 cp.wait()
         else:
-            remote(OB.at[xt], rows, o_s.at[k], o_r.at[sub], dst)
+            remote(OB.at[xt], rows, (o_s, (k,)), o_r.at[sub], dst)
     for q in range(4):
         piece = ig_out.at[pl.ds(q * 64, 64), :]
 
@@ -515,11 +616,24 @@
 
     for cp in local_out:
         cp.wait()
-    for when, cp in sends:
-        if when is None:
-            cp.wait_send()
+    def sent(size, ssem):
+        same = RED.at[0] if size == 1024 else WB.at[0, 0, pl.ds(0, size // 512)]
+        pltpu.make_async_remote_copy(
+            src_ref=same, dst_ref=same, send_sem=ssem[0].at[ssem[1]], recv_sem=o_r.at[0],
+            device_id=other, device_id_type=MESH,
+        ).wait_send()
+
+    for flag in (None, is_inner, is_outer, not_mine):
+        group = [entry[1:] for entry in sends if entry[0] is flag]
+
+        def drain(group=group):
+            for entry in group:
+                sent(*entry)
+
+        if flag is None:
+            drain()
         else:
-            pl.when(when)(cp.wait_send)
+            pl.when(flag)(drain)
 
 
 def whole_call(act, cot, wblk, lstat, rstat):
@@ -535,7 +649,7 @@
             pltpu.VMEM((4, 2, 4, 128, 512), bf),
             pltpu.VMEM((4, 128, 512), bf),
             pltpu.VMEM((4, 2, 4, 2, 64, 512), bf),
-            pltpu.VMEM((4, 4, 64, 1024), bf),
+            pltpu.VMEM((4, 4, 4, 16, 1024), bf),
             pltpu.VMEM((8, 2, 512, 512), bf),
             pltpu.VMEM((2, 256, 512), f32),
             pltpu.VMEM((4, 64, 1024), bf),
@@ -551,7 +665,7 @@
             pltpu.VMEM((19, 8, 128), f32),
             DMA((6,)), DMA((4,)), DMA((4,)), DMA((4,)), DMA((4,)),
             DMA((5, 4)), DMA((3, 4)), DMA((4, 4)), DMA((4, 4)),
-            DMA((3,)), DMA((3,)), DMA((2, 4)), DMA((2, 4)), DMA((18,)), DMA((18,)),
+            DMA((3,)), DMA((3,)), DMA((5, 4)), DMA((5, 4)), DMA((30,)), DMA((30,)),
             DMA((4,)), DMA((4,)), DMA((2, 5, 2)), DMA((2, 5, 2)), DMA((21,)), DMA((21,)),
             DMA((4,)), DMA((4,)), DMA((15,)), DMA((15,)), DMA((5,)),
         ],
@@ -560,6 +674,34 @@
         ),
         name="gather_products",
     )(act, cot, wblk, lstat, rstat)
+
+
+def copy_kernel(*refs):
+    n = (len(refs) - 2) // 3
+    src, dst, held = refs[:n], refs[n : 2 * n], refs[2 * n : 3 * n]
+    into = [pltpu.make_async_copy(src[i], held[i], refs[-2].at[i]) for i in range(n)]
+    out = [pltpu.make_async_copy(held[i], dst[i], refs[-1].at[i]) for i in range(n)]
+    for cp in into:
+        cp.start()
+    for i in range(n):
+        into[i].wait()
+        out[i].start()
+    for cp in out:
+        cp.wait()
+
+
+def place(*arrays):
+    any_spec = pl.BlockSpec(memory_space=pl.ANY)
+    n = len(arrays)
+    return pl.pallas_call(
+        copy_kernel,
+        out_shape=tuple(jax.ShapeDtypeStruct(a.shape, a.dtype) for a in arrays),
+        in_specs=[any_spec] * n,
+        out_specs=(any_spec,) * n,
+        scratch_shapes=[pltpu.VMEM(a.shape, a.dtype) for a in arrays] + [DMA((n,)), DMA((n,))],
+        compiler_params=pltpu.CompilerParams(vmem_limit_bytes=60 * 1024 * 1024),
+        name="place",
+    )(*arrays)
 
 
 def on_device(activations, cotangent, weight_blocks, left_stat, right_stat):
@@ -571,6 +713,9 @@
         left_stat.reshape(square),
         right_stat.reshape(square),
     )
+    input_grad, left_next, right_next, update = place(
+        input_grad, left_next, right_next, update
+    )
     shape_out = left_stat.shape
     return (
         input_grad,

time: 138 us -> 115 us (0.83)
  Pallas kernels: 130 us -> 114 us
  local copies, waits for them, and re-layouts: 6.25 us -> 0 us
    pallas_call x1, Pallas kernels: 130 us -> 110 us  [whole_call(): pl.pallas_call(whole_kernel, out_shape=(jax.ShapeDtypeStruct((256, 1024),...]
    unnamed x8 -> x0, local copies, waits for them, and re-layouts: 6.25 us -> none
    pallas_call x0 -> x1, Pallas kernels: none -> 3.18 us  [place(): pl.pallas_call(copy_kernel, out_shape=tuple((jax.ShapeDtypeStruct(a.shape...]
where the time goes in v3:
time: 115 us; the launch traced here: 114 us
  Pallas kernels  114 us (99%)
    pallas_call x1, Pallas kernels, whole_call(): pl.pallas_call(whole_kernel, out_shape=(jax.ShapeDtypeStruct((256, 1024),...  110 us
    pallas_call x1, Pallas kernels, place(): pl.pallas_call(copy_kernel, out_shape=tuple((jax.ShapeDtypeStruct(a.shape...  3.18 us

profile of v3, /device:TPU:32, one launch (start us, length us, event | category | flops | bytes accessed | tf_op | source)
XLA Modules:
  0.0 114.3 jit_solution(6941408270212421115)
XLA Ops:
  0.6 110.5 %gather_products.1 = (bf16[256,1024]{1,0:T(8,128)(2,1)}, f32[512,512]{1,0:T(8,128)}, f32[512,512]{1,0:T(8,128)}, f32[512,512]{1,0:T(8,128)}) custom-call(bf16[256,4096]{1,0:T(8,128)(2,1)} %act.1, bf16[256,1024]{1,0:T(8,128)(2,1)} %cot.1, bf16[512,512]{1,0:T(8,128)(2,1)} %bitcast.8, f32[512,512]{1,0:T(8,128)} %bitcast.6, f32[512,512]{1,0:T(8,128)} %bitcast.7), custom_call_target="tpu_custom_call" | custom-call | tf_op jit(solution)/shard_map/gather_products/pallas_call | solution.py:643
  111.1 3.2 %place.1 = (bf16[256,1024]{1,0:T(8,128)(2,1)}, f32[512,512]{1,0:T(8,128)}, f32[512,512]{1,0:T(8,128)}, f32[512,512]{1,0:T(8,128)}) custom-call(bf16[256,1024]{1,0:T(8,128)(2,1)} %get-tuple-element.12.refs_0_, f32[512,512]{1,0:T(8,128)} %get-tuple-element.13.refs_1_, f32[512,512]{1,0:T(8,128)} %get-tuple-element.14.refs_2_, f32[512,512]{1,0:T(8,128)} %get-tuple-element.15.refs_3_), custom_call_target="tpu_custom_call" | custom-call | tf_op jit(solution)/shard_map/place/pallas_call | solution.py:696

commit v4 on v3

--- a/solution.py
+++ b/solution.py
@@ -43,10 +43,10 @@
 def whole_kernel(
     act, cot, wblk, lstat, rstat,
     ig_out, left_out, right_out, update_out,
-    ACT, OUTB, COT, CIG, WB, ACC, OB, G, GS, STAT, T2, T3, MS, CS, PS, RAW, RED,
+    ACT, OUTB, COT, CIG, WB, ACC, OB, G, GS, STAT, T2, T3, MS, CS, PS, RAW, RED, HOP,
     loc_sem, a1_s, a1_r, a1o_s, a1o_r, tz_s, tz_r, sw_s, sw_r,
     b1_s, b1_r, pa_s, pa_r, ring_s, ring_r, c1_s, c1_r, w_s, w_r, ws_s, ws_r, o_s, o_r,
-    red_s, red_r, st_sem,
+    red_s, red_r, st_sem, hop_s, hop_r,
 ):
     dp = lax.axis_index("dp")
     y = lax.axis_index("mp")
@@ -92,11 +92,11 @@
     def greet(device):
         pl.semaphore_signal(barrier, inc=1, device_id=device, device_id_type=MESH)
 
-    for k in range(4):
-        for m in range(4):
-            if k or m:
-                greet({"dp": xp(k) * 4 + zh, "mp": y, "pre": lax.rem(pre + m, 4)})
-                count += 1
+    for k in range(1, 4):
+        greet({"dp": dp, "mp": y, "pre": lax.rem(pre + k, 4)})
+        greet(dev(xp(k), y, z, c))
+        greet(dev(xp(k), y, z, oc))
+        count += 3
     for k in range(1, 4):
         greet(dev(x, yp(k), z, c))
         count += 1
@@ -466,6 +466,51 @@
     local_out = []
     pltpu.make_async_copy(lstat, STAT.at[0], st_sem.at[0]).start()
     pltpu.make_async_copy(rstat, STAT.at[1], st_sem.at[1]).start()
+
+    sub = zl * 2 + c
+    z_to = zh * 2 + lax.div(x, 2)
+    z_pair = zh * 2 + 1 - zl
+    c_to = lax.rem(x, 2)
+    mine = pre == x
+    not_mine = jnp.logical_not(mine)
+    home = lax.div(x, 2) == zl
+    away = jnp.logical_not(home)
+    passing = x != 2 * (1 - zl) + c
+
+    def rows_of(n, part):
+        j = grp if part == 0 else 1 - grp
+        return ig_out.at[
+            pl.ds(pl.multiple_of(n * 64, 64), 64), pl.ds(pl.multiple_of(j * 512, 512), 512)
+        ]
+
+    def result_send(part):
+        j = grp if part == 0 else 1 - grp
+        OB[part] = ACC[j].reshape(4, 64, 512).astype(jnp.bfloat16)
+        rows = rows_of(sub, part)
+        for k in (3, 1, 2):
+            xt = xs[k]
+            dst = dev(xt, y, z, c_to)
+            remote(OB.at[part, xt], HOP.at[part, c], (hop_s, (part, k)), hop_r.at[part, c], dst,
+                   when=away)
+            remote(OB.at[part, xt], rows, (o_s, (part, k)), o_r.at[part, sub], dst, when=home)
+        remote(OB.at[part, x], rows, (o_s, (part, 0)), o_r.at[part, sub],
+               dev(x, y, z_to, c_to), when=not_mine)
+
+        @pl.when(mine)
+        def _():
+            cp = pltpu.make_async_copy(OB.at[part, x], rows, loc_sem.at[5])
+            cp.start()
+            cp.wait()
+
+    def result_pass(part):
+        for cc in range(2):
+            @pl.when(passing)
+            def _():
+                arrived(HOP.at[part, cc], hop_r.at[part, cc])
+
+            n = zl * 2 + cc
+            remote(HOP.at[part, cc], rows_of(n, part), (hop_s, (part, 4 + cc)), o_r.at[part, n],
+                   dev(x, y, z_pair, c), when=passing)
 
     cot_a(0)
     act_sends()
@@ -486,18 +531,18 @@
         near(0)
         far(2)
         cot_a(2)
-        cot_b(1)
         near(1)
         far(3)
+        cot_b(1)
+        near(2)
+        end(0)
         cot_f(0)
         cot_b(3)
-        near(2)
-        end(0)
-        cot_b(2)
         near(3)
         end(1)
+        cot_b(2)
+        end(2)
         cot_f(1)
-        end(2)
         end(3)
         cot_f(3)
         cot_f(2)
@@ -521,19 +566,19 @@
         near(1)
         far(0)
         cot_a(2)
-        cot_b(1)
         near(2)
         far(1)
-        cot_f(0)
         near(3)
-        cot_b(3)
+        cot_b(1)
         far(2)
         end(0)
-        cot_b(2)
+        cot_f(0)
+        cot_b(3)
         far(3)
         end(1)
+        cot_b(2)
+        end(2)
         cot_f(1)
-        end(2)
         end(3)
         cot_f(3)
         cot_f(2)
@@ -551,26 +596,26 @@
     cot_e(2)
     cig_b()
     gradient()
+    w_half(1, 0)
     statistic(0, NT, lstat, left_out)
     statistic(1, TN, rstat, right_out)
-    w_half(1, 0)
     root_1(0)
+    w_half(1, 1)
     root_2(0)
     root_3(0)
-    w_half(1, 1)
+    root_1(1)
+    w_half(2, 0)
     cig_f()
-    root_1(1)
     root_2(1)
     root_3(1)
     raw_1()
-    w_half(2, 0)
     raw_2()
     red_start(0)
     red_finish(0)
     red_start(1)
+    w_half(2, 1)
     cig_e()
     ig_own()
-    w_half(2, 1)
     red_finish(1)
     red_start(2)
     ig_step(1)
@@ -582,48 +627,30 @@
     red_finish(3)
     update()
     ig_step(3)
+    result_send(0)
     w_half(4, 0)
     w_half(4, 1)
+    result_pass(0)
     ig_step(4)
-
-    for j in range(2):
-        OB[:, :, pl.ds(j * 512, 512)] = ACC[j].reshape(4, 64, 512).astype(jnp.bfloat16)
-    sub = zl * 2 + c
-    z_to = zh * 2 + lax.div(x, 2)
-    c_to = lax.rem(x, 2)
-    rows = ig_out.at[pl.ds(pl.multiple_of(sub * 64, 64), 64), :]
-    mine = pre == x
-    not_mine = jnp.logical_not(mine)
-    for k in range(4):
-        xt = xs[k]
-        dst = dev(xt, y, z_to, c_to)
-        if k == 0:
-            remote(OB.at[xt], rows, (o_s, (k,)), o_r.at[sub], dst, when=not_mine)
-
-            @pl.when(mine)
-            def _():
-                cp = pltpu.make_async_copy(OB.at[x], rows, loc_sem.at[5])
-                cp.start()
-                cp.wait()
-        else:
-            remote(OB.at[xt], rows, (o_s, (k,)), o_r.at[sub], dst)
+    result_send(1)
+    result_pass(1)
+
     for q in range(4):
-        piece = ig_out.at[pl.ds(q * 64, 64), :]
-
         @pl.when(jnp.logical_not(jnp.logical_and(mine, sub == q)))
         def _():
-            arrived(piece, o_r.at[q])
+            for part in range(2):
+                arrived(rows_of(q, part), o_r.at[part, q])
 
     for cp in local_out:
         cp.wait()
     def sent(size, ssem):
         same = RED.at[0] if size == 1024 else WB.at[0, 0, pl.ds(0, size // 512)]
         pltpu.make_async_remote_copy(
-            src_ref=same, dst_ref=same, send_sem=ssem[0].at[ssem[1]], recv_sem=o_r.at[0],
+            src_ref=same, dst_ref=same, send_sem=ssem[0].at[ssem[1]], recv_sem=o_r.at[0, 0],
             device_id=other, device_id_type=MESH,
         ).wait_send()
 
-    for flag in (None, is_inner, is_outer, not_mine):
+    for flag in (None, is_inner, is_outer, not_mine, home, away, passing):
         group = [entry[1:] for entry in sends if entry[0] is flag]
 
         def drain(group=group):
@@ -652,7 +679,7 @@
             pltpu.VMEM((4, 4, 4, 16, 1024), bf),
             pltpu.VMEM((8, 2, 512, 512), bf),
             pltpu.VMEM((2, 256, 512), f32),
-            pltpu.VMEM((4, 64, 1024), bf),
+            pltpu.VMEM((2, 4, 64, 512), bf),
             pltpu.VMEM((BLOCK, BLOCK), f32),
             pltpu.VMEM((2, BLOCK, BLOCK), bf),
             pltpu.VMEM((2, BLOCK, BLOCK), f32),
@@ -663,11 +690,12 @@
             pltpu.VMEM((2, 2, BLOCK, BLOCK), bf),
             pltpu.VMEM((BLOCK, BLOCK), f32),
             pltpu.VMEM((19, 8, 128), f32),
+            pltpu.VMEM((2, 2, 64, 512), bf),
             DMA((6,)), DMA((4,)), DMA((4,)), DMA((4,)), DMA((4,)),
             DMA((5, 4)), DMA((3, 4)), DMA((4, 4)), DMA((4, 4)),
             DMA((3,)), DMA((3,)), DMA((5, 4)), DMA((5, 4)), DMA((30,)), DMA((30,)),
             DMA((4,)), DMA((4,)), DMA((2, 5, 2)), DMA((2, 5, 2)), DMA((21,)), DMA((21,)),
-            DMA((4,)), DMA((4,)), DMA((15,)), DMA((15,)), DMA((5,)),
+            DMA((2, 4)), DMA((2, 4)), DMA((15,)), DMA((15,)), DMA((5,)), DMA((2, 6)), DMA((2, 2)),
         ],
         compiler_params=pltpu.CompilerParams(
             collective_id=0, has_side_effects=True, vmem_limit_bytes=60 * 1024 * 1024

time: 115 us -> 107 us (0.930); the launches traced: 114 us -> 105 us
  Pallas kernels: 114 us -> 104 us
    pallas_call x1, Pallas kernels: 110 us -> 101 us  [whole_call(): pl.pallas_call(whole_kernel, out_shape=(jax.ShapeDtypeStruct((256, 1024),...]
where the time goes in v4:
time: 107 us; the launch traced here: 105 us
  Pallas kernels  104 us (97%)
    pallas_call x1, Pallas kernels, whole_call(): pl.pallas_call(whole_kernel, out_shape=(jax.ShapeDtypeStruct((256, 1024),...  101 us
    pallas_call x1, Pallas kernels, place(): pl.pallas_call(copy_kernel, out_shape=tuple((jax.ShapeDtypeStruct(a.shape...  3.18 us

profile of v4, /device:TPU:32, one launch (start us, length us, event | category | flops | bytes accessed | tf_op | source)
XLA Modules:
  0.0 105.1 jit_solution(14168582061594759351)
XLA Ops:
  0.6 101.2 %gather_products.1 = (bf16[256,1024]{1,0:T(8,128)(2,1)}, f32[512,512]{1,0:T(8,128)}, f32[512,512]{1,0:T(8,128)}, f32[512,512]{1,0:T(8,128)}) custom-call(bf16[256,4096]{1,0:T(8,128)(2,1)} %act.1, bf16[256,1024]{1,0:T(8,128)(2,1)} %cot.1, bf16[512,512]{1,0:T(8,128)(2,1)} %bitcast.8, f32[512,512]{1,0:T(8,128)} %bitcast.6, f32[512,512]{1,0:T(8,128)} %bitcast.7), custom_call_target="tpu_custom_call" | custom-call | tf_op jit(solution)/shard_map/gather_products/pallas_call | solution.py:670
  101.9 3.2 %place.1 = (bf16[256,1024]{1,0:T(8,128)(2,1)}, f32[512,512]{1,0:T(8,128)}, f32[512,512]{1,0:T(8,128)}, f32[512,512]{1,0:T(8,128)}) custom-call(bf16[256,1024]{1,0:T(8,128)(2,1)} %get-tuple-element.12.refs_0_, f32[512,512]{1,0:T(8,128)} %get-tuple-element.13.refs_1_, f32[512,512]{1,0:T(8,128)} %get-tuple-element.14.refs_2_, f32[512,512]{1,0:T(8,128)} %get-tuple-element.15.refs_3_), custom_call_target="tpu_custom_call" | custom-call | tf_op jit(solution)/shard_map/place/pallas_call | solution.py:724

commit v5 on v4

--- a/solution.py
+++ b/solution.py
@@ -624,10 +624,10 @@
     red_start(3)
     ig_step(2)
     w_half(3, 1)
+    ig_step(3)
+    result_send(0)
     red_finish(3)
     update()
-    ig_step(3)
-    result_send(0)
     w_half(4, 0)
     w_half(4, 1)
     result_pass(0)

time: 107 us -> 105 us (0.981)
    pallas_call x1, Pallas kernels: 101 us -> 99.9 us  [whole_call(): pl.pallas_call(whole_kernel, out_shape=(jax.ShapeDtypeStruct((256, 1024),...]
where the time goes in v5:
time: 105 us; the launch traced here: 104 us
  Pallas kernels  103 us (98%)
    pallas_call x1, Pallas kernels, whole_call(): pl.pallas_call(whole_kernel, out_shape=(jax.ShapeDtypeStruct((256, 1024),...  99.9 us
    pallas_call x1, Pallas kernels, place(): pl.pallas_call(copy_kernel, out_shape=tuple((jax.ShapeDtypeStruct(a.shape...  3.18 us

profile of v5, /device:TPU:32, one launch (start us, length us, event | category | flops | bytes accessed | tf_op | source)
XLA Modules:
  0.0 103.7 jit_solution(6825490838741347954)
XLA Ops:
  0.6 99.9 %gather_products.1 = (bf16[256,1024]{1,0:T(8,128)(2,1)}, f32[512,512]{1,0:T(8,128)}, f32[512,512]{1,0:T(8,128)}, f32[512,512]{1,0:T(8,128)}) custom-call(bf16[256,4096]{1,0:T(8,128)(2,1)} %act.1, bf16[256,1024]{1,0:T(8,128)(2,1)} %cot.1, bf16[512,512]{1,0:T(8,128)(2,1)} %bitcast.8, f32[512,512]{1,0:T(8,128)} %bitcast.6, f32[512,512]{1,0:T(8,128)} %bitcast.7), custom_call_target="tpu_custom_call" | custom-call | tf_op jit(solution)/shard_map/gather_products/pallas_call | solution.py:670
  100.5 3.2 %place.1 = (bf16[256,1024]{1,0:T(8,128)(2,1)}, f32[512,512]{1,0:T(8,128)}, f32[512,512]{1,0:T(8,128)}, f32[512,512]{1,0:T(8,128)}) custom-call(bf16[256,1024]{1,0:T(8,128)(2,1)} %get-tuple-element.12.refs_0_, f32[512,512]{1,0:T(8,128)} %get-tuple-element.13.refs_1_, f32[512,512]{1,0:T(8,128)} %get-tuple-element.14.refs_2_, f32[512,512]{1,0:T(8,128)} %get-tuple-element.15.refs_3_), custom_call_target="tpu_custom_call" | custom-call | tf_op jit(solution)/shard_map/place/pallas_call | solution.py:724
